TPU v7x, 128 devices: a whole 4x4x4 slice. The times are simulated.
128 devices in a mesh: deg: 16 (over y, x_hi, core), row: 8 (over z, x_lo).
Axes of the slice: x: 4 (x_hi: 2, x_lo: 2; x = x_hi * 2 + x_lo), y: 4, z: 4, core: 2. Of those that a mesh axis runs over, the one named last changes fastest.
Arguments:
- left: float32 [16384, 4096], P('deg', 'row'), may hold values from 0 to 7340032, as said below
- right: float32 [16384, 1024], P('deg', 'row'), may hold values from 0 to 7340032, as said below
Outputs:
- product_scaled: float32 [32768, 1024], P('deg', 'row')
Inputs may be any that keep to these rules, and one draw needn't show every extreme that they name: `left`: every entry is an integer residue modulo the prime 7340033. `right`: every entry is an integer residue modulo the prime 7340033.
All inputs are finite; a program needn't handle non-finite values.
Results may differ from a plain program's by a relative error of at most 0.0003.
Values sent between devices are 32-bit elements; how exact they have to be, the bound alone decides.
No kernel may reach another device: no remote copies, remote signals or barrier semaphores. Data moves between devices by JAX's collectives and lax.ppermute only.
A program may use at most 256 MiB of HBM per device.

v0:
```python
import jax
import jax.numpy as jnp
import numpy as np
from jax import lax
from jax.sharding import PartitionSpec as P

DEG = 16384
K = 64
COLS = 16
ROWS_DEV = 8


modulus = 7340033
inv_modulus = 1.0 / 7340033.0
generator = 3


def power_list(unit_root, entries):
    values = np.ones(entries, dtype=np.int64)
    current = 1
    for position in range(entries):
        values[position] = current
        current = current * unit_root % modulus
    return values


def root_of(period, inverse):
    element = pow(generator, (modulus - 1) // period, modulus)
    return pow(element, modulus - 2, modulus) if inverse else element


def add_mod(first, second):
    summed = first + second
    return jnp.where(summed >= modulus, summed - modulus, summed)


def sub_mod(first, second):
    differ = first - second
    return jnp.where(differ < 0, differ + modulus, differ)


def mul_mod(first, second):
    quotient = jnp.floor(first * second * inv_modulus)
    residual = (
        first.astype(jnp.int32) * second.astype(jnp.int32) - quotient.astype(jnp.int32) * modulus
    )
    return jnp.remainder(residual, modulus).astype(first.dtype)


def transform(values, dimension, unit_root):
    length = values.shape[dimension]
    powers = power_list(unit_root, length)
    leading = values.shape[:dimension]
    trailing = values.shape[dimension + 1 :]
    current = values.reshape(leading + (1, length) + trailing)
    stride = 1
    while stride < length:
        half_size = current.shape[dimension + 1] // 2
        even_part = lax.slice_in_dim(current, 0, half_size, axis=dimension + 1)
        odd_part = lax.slice_in_dim(current, half_size, 2 * half_size, axis=dimension + 1)
        factor = powers[length // (2 * stride) * np.arange(stride)]
        factor = jnp.asarray(factor, dtype=jnp.float32).reshape(
            (1,) * len(leading) + (stride, 1) + (1,) * len(trailing)
        )
        twisted = mul_mod(odd_part, factor)
        current = jnp.concatenate(
            [add_mod(even_part, twisted), sub_mod(even_part, twisted)], axis=dimension
        )
        stride = stride * 2
    return current.reshape(leading + (length,) + trailing)


def digits_of(values):
    high_digit = jnp.floor(values * (1.0 / 65536.0))
    remaining = values - high_digit * 65536.0
    middle = jnp.floor(remaining * (1.0 / 256.0))
    low_digit = remaining - middle * 256.0
    return (low_digit, middle, high_digit)


def fold_sums(digit_sums):
    combined = None
    for shift in range(5):
        weight = jnp.asarray(float(pow(2, 8 * shift, modulus)), dtype=jnp.float32)
        scaled_term = mul_mod(digit_sums[shift], weight)
        combined = scaled_term if combined is None else add_mod(combined, scaled_term)
    return combined


def digit_products(left_digits, right_digits, digit_sums):
    updated = list(digit_sums)
    for first_digit in range(3):
        for second_digit in range(3):
            updated[first_digit + second_digit] = updated[first_digit + second_digit] + jnp.einsum(
                "prk,pkc->prc",
                left_digits[first_digit],
                right_digits[second_digit],
                preferred_element_type=jnp.float32,
            )
    return tuple(updated)


def on_device(left, right):
    coef_rows = left.shape[0]
    groups_deg = lax.axis_size("deg")
    mine = lax.axis_index("deg")
    length = 2 * DEG
    points_block = coef_rows // groups_deg
    forward_table = jnp.asarray(power_list(root_of(length, False), length), dtype=jnp.float32)
    backward_table = jnp.asarray(power_list(root_of(length, True), length), dtype=jnp.float32)
    scale_back = jnp.asarray(float(pow(length, modulus - 2, modulus)), dtype=jnp.float32)
    spread = (
        lax.all_to_all(
            left.reshape(1, coef_rows, -1), "deg", split_axis=1, concat_axis=0, tiled=True
        ),
        lax.all_to_all(
            right.reshape(1, coef_rows, -1), "deg", split_axis=1, concat_axis=0, tiled=True
        ),
    )
    positions = mine * points_block + jnp.arange(points_block, dtype=jnp.int32)
    freqs = jnp.arange(2 * groups_deg, dtype=jnp.int32)
    twiddle = jnp.take(forward_table, freqs[:, None] * positions[None, :] % length)
    small_root = root_of(2 * groups_deg, False)

    def forward_local(block):
        padded = jnp.concatenate([block, jnp.zeros_like(block)], axis=0)
        return mul_mod(transform(padded, 0, small_root), twiddle[:, :, None])

    mixed = (
        lax.all_to_all(forward_local(spread[0]), "deg", split_axis=0, concat_axis=1, tiled=True),
        lax.all_to_all(forward_local(spread[1]), "deg", split_axis=0, concat_axis=1, tiled=True),
    )
    block_root = root_of(coef_rows, False)
    left_eval = transform(mixed[0], 1, block_root)
    right_eval = transform(mixed[1], 1, block_root)
    left_digits = [
        digit.astype(jnp.bfloat16)
        for digit in digits_of(left_eval.reshape(2 * coef_rows, ROWS_DEV, K))
    ]
    empty = tuple((jnp.zeros((2 * coef_rows, ROWS_DEV, COLS), jnp.float32) for shift in range(5)))
    piece = lax.all_gather(right_eval, "row", axis=2, tiled=True)
    inner = piece.shape[2] // COLS
    piece_digits = [
        digit.astype(jnp.bfloat16) for digit in digits_of(piece.reshape(2 * coef_rows, inner, COLS))
    ]
    chosen = [digit for digit in left_digits]
    digit_sums = digit_products(chosen, piece_digits, empty)
    product = fold_sums(digit_sums).reshape(2, coef_rows, ROWS_DEV * COLS)
    back_eval = transform(product, 1, root_of(coef_rows, True))
    pairs = 2 * mine + jnp.arange(2, dtype=jnp.int32)
    offsets = jnp.arange(coef_rows, dtype=jnp.int32)
    back_twiddle = mul_mod(
        jnp.take(backward_table, pairs[:, None] * offsets[None, :] % length), scale_back
    )
    scaled = mul_mod(back_eval, back_twiddle[:, :, None])
    spread_back = lax.all_to_all(scaled, "deg", split_axis=1, concat_axis=0, tiled=True)
    coefficients = transform(spread_back, 0, root_of(2 * groups_deg, True))
    result = lax.all_to_all(coefficients, "deg", split_axis=0, concat_axis=1, tiled=True)
    return result.reshape(2 * coef_rows, -1) / 7340033.0


def solution(mesh):
    return jax.shard_map(
        on_device,
        mesh=mesh,
        in_specs=(P("deg", "row"), P("deg", "row")),
        out_specs=P("deg", "row"),
        check_vma=False,
    )
```

profile of v0, /device:TPU:1, one launch (start us, length us, event | category | flops | bytes accessed | tf_op | source)
XLA Modules:
  0.0 696.0 jit_solution(17654048473712545252)
XLA Ops:
  6.5 8.6 %all-to-all-start.2 = ((f32[1,1024,128]{2,0,1:T(1,128)}), f32[1,1024,128]{2,0,1:T(1,128)S(1)}, u32[]{:S(2)}, u32[]{:S(2)}) async-start(f32[1,1024,128]{2,0,1:T(1,128)} %bitcast.112), calls=%async_computation.2 | async-start | bytes 1048576 | tf_op jit(solution)/shard_map/all_to_all | solution.py:116
  15.2 11.8 %gather_fusion = f32[2048]{0:T(1024)S(1)} fusion(f32[32768]{0:T(1024)S(1)} %copy-done, s32[2048]{0:T(1024)S(1)} %broadcast_clamp_fusion), kind=kCustom, calls=%fused_computation | custom fusion | bytes 24576 | tf_op jit(solution)/shard_map/jit(_take)/gather | solution.py:122
  32.4 7.2 %all-to-all-start.3 = ((f32[32,64,128]{2,1,0:T(8,128)}), f32[32,64,128]{2,1,0:T(8,128)S(1)}, u32[]{:S(2)}, u32[]{:S(2)}) async-start(f32[32,64,128]{2,1,0:T(8,128)} %fusion.40), calls=%async_computation.3 | async-start | bytes 2097152 | tf_op jit(solution)/shard_map/all_to_all | solution.py:131
  42.4 14.5 %all-to-all-done.3 = f32[32,64,128]{2,1,0:T(8,128)S(1)} async-done(((f32[32,64,128]{2,1,0:T(8,128)}), f32[32,64,128]{2,1,0:T(8,128)S(1)}, u32[]{:S(2)}, u32[]{:S(2)}) %all-to-all-start.3) | async-done | bytes 1048608 | tf_op jit(solution)/shard_map/all_to_all | solution.py:131
  69.9 23.1 %all-to-all-done = f32[1,1024,512]{2,0,1:T(1,128)S(1)} async-done(((f32[1,1024,512]{2,0,1:T(1,128)}), f32[1,1024,512]{2,0,1:T(1,128)S(1)}, u32[]{:S(2)}, u32[]{:S(2)}) %all-to-all-start) | async-done | bytes 2097184 | tf_op jit(solution)/shard_map/all_to_all | solution.py:113
  105.6 11.2 %compare_select_fusion.6 = (f32[8,2,64,512]{3,1,2,0:T(2,128)S(1)}, f32[8,2,64,512]{3,1,2,0:T(2,128)S(1)}) fusion(f32[4,4,64,512]{3,1,2,0:T(4,128)S(1)} %compare_select_fusion.24, f32[4,4,64,512]{3,1,2,0:T(4,128)S(1)} %get-tuple-element.34, f32[8]{0:T(128)S(1)} %copy-done.7, s32[8]{0:T(128)S(1)} %copy-done.8), kind=kLoop, calls=%fused_computation.22 | loop fusion | flops 11010048 | bytes 8388672 | tf_op jit(solution)/shard_map/jit(_where)/select_n | solution.py:39
  118.9 23.6 %compare_select_fusion.3 = (f32[16,1,64,512]{3,1,2,0:T(1,128)}, f32[16,1,64,512]{3,1,2,0:T(1,128)S(1)}, f32[16,1,64,512]{3,1,2,0:T(1,128)S(1)}) fusion(f32[16]{0:T(128)S(1)} %copy-done.5, s32[16]{0:T(128)S(1)} %copy-done.6, f32[8,2,64,512]{3,1,2,0:T(2,128)S(1)} %get-tuple-element.32, f32[8,2,64,512]{3,1,2,0:T(2,128)S(1)} %compare_select_fusion.7), kind=kLoop, calls=%fused_computation.11 | loop fusion | flops 11010048 | bytes 10485888 | tf_op jit(solution)/shard_map/jit(_where)/select_n | solution.py:34
  146.1 8.7 %pad_maximum_fusion = f32[32,1,64,512]{3,1,2,0:T(1,128)} fusion(f32[16,1,64,512]{3,1,2,0:T(1,128)S(1)} %compare_select_fusion.2, f32[16,1,64,512]{3,1,2,0:T(1,128)} %get-tuple-element.29), kind=kLoop, calls=%fused_computation.56 | loop fusion | flops 1048576 | bytes 8388608 | tf_op jit(solution)/shard_map/concatenate | solution.py:66
  154.8 6.8 fusion.4
  168.2 11.8 %gather_fusion.1 = f32[2048]{0:T(1024)S(1)} fusion(f32[32768]{0:T(1024)S(1)} %copy-done.1, s32[2048]{0:T(1024)S(1)} %bitcast_clamp_fusion), kind=kCustom, calls=%fused_computation.1 | custom fusion | bytes 24576 | tf_op jit(solution)/shard_map/jit(_take)/gather | solution.py:153
  180.8 83.5 %all-to-all-done.1 = f32[32,64,512]{2,1,0:T(8,128)} async-done(((f32[32,64,512]{2,1,0:T(8,128)}), f32[32,64,512]{2,1,0:T(8,128)}, u32[]{:S(2)}, u32[]{:S(2)}) %all-to-all-start.1) | async-done | bytes 4194336 | tf_op jit(solution)/shard_map/all_to_all | solution.py:130
  267.5 17.2 %compare_select_fusion.1 = (f32[2,1,512,512]{3,1,2,0:T(1,128)S(1)}, f32[2,1,512,512]{3,1,2,0:T(1,128)S(1)}) fusion(f32[2,1,512,512]{3,2,0,1:T(8,128)S(1)} %get-tuple-element.53, f32[2,1,512,512]{3,2,0,1:T(8,128)S(1)} %get-tuple-element.52), kind=kLoop, calls=%fused_computation.9 | loop fusion | flops 8912896 | bytes 8388608 | tf_op jit(solution)/shard_map/jit(_where)/select_n | solution.py:34
  284.7 6.8 compare_select_fusion
  291.5 11.2 %compare_select_fusion.5 = (f32[2,2,256,512]{3,1,2,0:T(2,128)S(1)}, f32[2,2,256,512]{3,1,2,0:T(2,128)S(1)}) fusion(f32[2,1,512,512]{3,1,2,0:T(1,128)S(1)} %compare_select_fusion, f32[2,1,512,512]{3,1,2,0:T(1,128)S(1)} %get-tuple-element.25, f32[2]{0:T(128)S(1)} %copy-done.11, s32[2]{0:T(128)S(1)} %copy-done.12), kind=kLoop, calls=%fused_computation.19 | loop fusion | flops 11010048 | bytes 8388624 | tf_op jit(solution)/shard_map/jit(_where)/select_n | solution.py:34
  336.3 7.1 %reshape.589 = f32[2048,8,64]{2,1,0:T(8,128)} reshape(f32[2,1024,1,512]{3,1,2,0:T(8,128)} %pad_maximum_fusion.1) | data formatting | bytes 8388608 | tf_op jit(solution)/shard_map/reshape;reshape | solution.py:138
  343.4 13.3 %copy.366 = f32[2,1024,1,1024]{1,0,3,2:T(2,128)} copy(f32[2,1024,1,1024]{3,1,2,0:T(8,128)} %all-gather.3.cloned.1.call-done) | data formatting | bytes 16777216 | tf_op jit(solution)/shard_map/all_gather | solution.py:141
  356.7 11.8 %reshape.565 = f32[2048,64,16]{0,2,1:T(8,128)} reshape(f32[2,1024,1,1024]{1,0,3,2:T(2,128)} %copy.366) | data formatting | bytes 16777216 | tf_op jit(solution)/shard_map/reshape | solution.py:144
  368.5 15.5 %copy.368 = f32[2048,64,16]{1,2,0:T(8,128)} copy(f32[2048,64,16]{0,2,1:T(8,128)} %reshape.565) | data formatting | bytes 16777216 | tf_op jit(solution)/shard_map/reshape | solution.py:144
  384.0 11.2 %subtract_convert_fusion = bf16[2048,64,16]{1,2,0:T(8,128)(2,1)} fusion(f32[2048,64,16]{1,2,0:T(8,128)} %copy.368), kind=kLoop, calls=%fused_computation.2 | loop fusion | flops 18874368 | bytes 12582912 | tf_op jit(solution)/shard_map/convert_element_type | solution.py:144
  395.3 13.5 %fusion.136 = f32[2048,8,16]{2,1,0:T(8,128)} fusion(bf16[2048,64,16]{1,2,0:T(8,128)(2,1)} %subtract_convert_fusion, f32[2048,8,64]{2,1,0:T(8,128)} %reshape.589), kind=kOutput, calls=%fused_computation.499 | convolution fusion | flops 42991616 | bytes 9437184 | tf_op jit(solution)/shard_map/prk,pkc->prc/dot_general | solution.py:94
  408.8 13.5 %fusion.133 = f32[2048,8,16]{2,1,0:T(8,128)} fusion(bf16[2048,64,16]{1,2,0:T(8,128)(2,1)} %subtract_convert_fusion, f32[2048,8,64]{2,1,0:T(8,128)} %reshape.589), kind=kOutput, calls=%fused_computation.497 | convolution fusion | flops 40894464 | bytes 9437184 | tf_op jit(solution)/shard_map/prk,pkc->prc/dot_general | solution.py:94
  422.4 13.2 %fusion.135 = f32[2048,8,16]{2,1,0:T(8,128)} fusion(f32[2048,8,64]{2,1,0:T(8,128)} %reshape.589, f32[2048,64,16]{1,2,0:T(8,128)} %copy.368), kind=kOutput, calls=%fused_computation.498 | convolution fusion | flops 57671680 | bytes 13631488 | tf_op jit(solution)/shard_map/prk,pkc->prc/dot_general | solution.py:94
  435.6 13.1 %fusion.131 = f32[2048,8,16]{2,1,0:T(8,128)} fusion(f32[2048,8,64]{2,1,0:T(8,128)} %reshape.589, f32[2048,64,16]{1,2,0:T(8,128)} %copy.368), kind=kOutput, calls=%fused_computation.496 | convolution fusion | flops 55574528 | bytes 13631488 | tf_op jit(solution)/shard_map/prk,pkc->prc/dot_general | solution.py:94
  448.7 13.0 %fusion.128 = f32[2048,8,16]{2,1,0:T(8,128)} fusion(f32[2048,64,16]{1,2,0:T(8,128)} %copy.368, f32[2048,8,64]{2,1,0:T(8,128)} %reshape.589), kind=kOutput, calls=%fused_computation.495 | convolution fusion | flops 49283072 | bytes 13631488 | tf_op jit(solution)/shard_map/prk,pkc->prc/dot_general | solution.py:94
  461.7 13.5 %fusion.123 = f32[2048,8,16]{2,1,0:T(8,128)} fusion(bf16[2048,64,16]{1,2,0:T(8,128)(2,1)} %subtract_convert_fusion, f32[2048,8,64]{2,1,0:T(8,128)} %reshape.589), kind=kOutput, calls=%fused_computation.493 | convolution fusion | flops 36700160 | bytes 9437184 | tf_op jit(solution)/shard_map/prk,pkc->prc/dot_general | solution.py:94
  475.1 13.3 %fusion.121 = f32[2048,8,16]{2,1,0:T(8,128)} fusion(f32[2048,8,64]{2,1,0:T(8,128)} %reshape.589, f32[2048,64,16]{1,2,0:T(8,128)} %copy.368), kind=kOutput, calls=%fused_computation.492 | convolution fusion | flops 51380224 | bytes 13631488 | tf_op jit(solution)/shard_map/prk,pkc->prc/dot_general | solution.py:94
  488.5 14.0 %fusion.126 = f32[2048,8,16]{2,1,0:T(8,128)} fusion(f32[2048,64,16]{1,2,0:T(8,128)} %copy.368, f32[2048,8,64]{2,1,0:T(8,128)} %reshape.589), kind=kOutput, calls=%fused_computation.494 | convolution fusion | flops 47185920 | bytes 13631488 | tf_op jit(solution)/shard_map/prk,pkc->prc/dot_general | solution.py:94
  502.5 13.8 %fusion.119 = f32[2048,8,16]{2,1,0:T(8,128)} fusion(f32[2048,8,64]{2,1,0:T(8,128)S(1)} %bitcast.91, f32[2048,64,16]{1,2,0:T(8,128)} %copy.368), kind=kOutput, calls=%fused_computation.491 | convolution fusion | flops 42991616 | bytes 13631488 | tf_op jit(solution)/shard_map/prk,pkc->prc/dot_general | solution.py:94
  568.1 7.5 %compare_select_fusion.30 = f32[2048,8,16]{0,2,1:T(8,128)} fusion(f32[2048,8,16]{0,2,1:T(8,128)} %copy.378, f32[2048,8,16]{0,2,1:T(8,128)} %copy.376, f32[2048,8,16]{0,2,1:T(8,128)} %copy.377, f32[2048,8,16]{0,2,1:T(8,128)} %copy.375, f32[2048,8,16]{0,2,1:T(8,128)} %copy.373, f32[2048,8,16]{0,2,1:T(8,128)} %copy.374, f32[2048,8,16]{0,2,1:T(8,128)S(1)} %copy.371, ...), kind=kLoop, calls=%fused_computation.99 | loop fusion | flops 23330816 | bytes 10485760 | tf_op jit(solution)/shard_map/jit(_where)/select_n | solution.py:34
  588.7 20.4 %all_to_all.78 = f32[2,1024,128]{2,0,1:T(2,128)S(1)} all-to-all(f32[2,1024,128]{2,0,1:T(2,128)S(1)} %copy.388), channel_id=1, replica_groups=mesh['deg'=16,'row'=8] {'deg'}, dimensions={1} | all-to-all | bytes 2097152 | tf_op jit(solution)/shard_map/all_to_all | solution.py:156
  619.1 42.4 %subtract_remainder_fusion.18 = s32[16,1,64,128]{3,1,2,0:T(1,128)S(1)} fusion(s32[16,1,64,128]{3,1,2,0:T(1,128)S(1)} %bitcast.106, f32[16,1,64,128]{3,1,2,0:T(1,128)S(1)} %bitcast.105, f32[8,2,64,128]{3,1,2,0:T(2,128)S(1)} %copy_select_fusion.2, f32[8,2,64,128]{3,1,2,0:T(2,128)S(1)} %copy.426, f32[16]{0:T(128)S(1)} %copy-done.23, s32[16]{0:T(128)S(1)} %copy-done.24), kind=kLoop, calls=%fused_computation.411 | loop fusion | flops 1310720 | bytes 2621568 | tf_op jit(solution)/shard_map/jit(remainder)/rem | solution.py:47
  667.1 20.6 %all_to_all.79 = f32[32,64,128]{2,1,0:T(8,128)S(1)} all-to-all(f32[32,64,128]{2,1,0:T(8,128)S(1)} %bitcast.101), channel_id=1, replica_groups=mesh['deg'=16,'row'=8] {'deg'}, dimensions={0} | all-to-all | bytes 2097152 | tf_op jit(solution)/shard_map/all_to_all | solution.py:158
  (212 shorter events, 164.1 us)
Async XLA Ops:
  6.5 8.7 %copy-start = (f32[32768]{0:T(1024)S(1)}, f32[32768]{0:T(1024)}, u32[]{:S(2)}) copy-start(f32[32768]{0:T(1024)} %constant.580.clone) | copy-start | bytes 393220
  6.5 20.6 %all-to-all-start.2 = ((f32[1,1024,128]{2,0,1:T(1,128)}), f32[1,1024,128]{2,0,1:T(1,128)S(1)}, u32[]{:S(2)}, u32[]{:S(2)}) async-start(f32[1,1024,128]{2,0,1:T(1,128)} %bitcast.112), calls=%async_computation.2 | async-start | bytes 1048576 | tf_op jit(solution)/shard_map/all_to_all | solution.py:116
  27.9 1.4 copy-start.7
  27.9 1.4 copy-start.8
  28.6 1.3 copy-start.5
  30.6 9.1 %copy-start.2 = (f32[1024,512]{1,0:T(8,128)S(1)}, f32[1024,512]{1,0:T(8,128)}, u32[]{:S(2)}) copy-start(f32[1024,512]{1,0:T(8,128)} %param.49) | copy-start | bytes 6291460
  32.4 24.4 %all-to-all-start.3 = ((f32[32,64,128]{2,1,0:T(8,128)}), f32[32,64,128]{2,1,0:T(8,128)S(1)}, u32[]{:S(2)}, u32[]{:S(2)}) async-start(f32[32,64,128]{2,1,0:T(8,128)} %fusion.40), calls=%async_computation.3 | async-start | bytes 2097152 | tf_op jit(solution)/shard_map/all_to_all | solution.py:131
  56.9 36.2 %all-to-all-start = ((f32[1,1024,512]{2,0,1:T(1,128)}), f32[1,1024,512]{2,0,1:T(1,128)S(1)}, u32[]{:S(2)}, u32[]{:S(2)}) async-start(f32[1,1024,512]{2,0,1:T(1,128)} %reshape.556), calls=%async_computation | async-start | bytes 4194304 | tf_op jit(solution)/shard_map/all_to_all | solution.py:113
  61.3 282.1 %all-gather.3.cloned.1.call-start = ((), (), s32[]{:S(2)}) async-start(), calls=%async_computation.6 | async-start | bytes 9437184 | tf_op jit(solution)/shard_map/all_gather | solution.py:141
  64.8 1.4 copy-start.29
  64.8 1.4 copy-start.30
  65.4 1.4 copy-start.27
  65.5 1.4 copy-start.28
  66.1 1.4 copy-start.17
  66.2 1.4 copy-start.18
  66.8 1.4 copy-start.13
  66.8 1.3 copy-start.14
  161.6 6.6 copy-start.1
  161.6 102.7 %all-to-all-start.1 = ((f32[32,64,512]{2,1,0:T(8,128)}), f32[32,64,512]{2,1,0:T(8,128)}, u32[]{:S(2)}, u32[]{:S(2)}) async-start(f32[32,64,512]{2,1,0:T(8,128)} %fusion.4), calls=%async_computation.1 | async-start | bytes 8388608 | tf_op jit(solution)/shard_map/all_to_all | solution.py:130
  475.1 27.4 %slice-start = ((s8[8388608]{0:T(1024)(128)(4,1)}), s8[4194304]{0:T(1024)(128)(4,1)S(1)}, s32[]{:S(2)}) async-start(s8[8388608]{0:T(1024)(128)(4,1)} %bitcast.90), calls=%async_computation.7 | async-start | bytes 8388608
  488.5 14.0 %slice-start.1 = ((s8[8388608]{0:T(1024)(128)(4,1)}), s8[4194304]{0:T(1024)(128)(4,1)S(1)}, s32[]{:S(2)}) async-start(s8[8388608]{0:T(1024)(128)(4,1)} %bitcast.90), calls=%async_computation.8 | async-start | bytes 8388608
  579.2 1.3 copy-start.19
  582.5 1.4 copy-start.37
  582.5 1.4 copy-start.38
  583.2 1.4 copy-start.35
  583.2 1.4 copy-start.36
  583.9 1.4 copy-start.33
  583.9 1.4 copy-start.34
  584.6 1.4 copy-start.21
  584.6 1.4 copy-start.22
  585.3 1.3 copy-start.3
  585.3 1.3 copy-start.4
  (16 other events, 19.2 us)
Sparse Core Ops, SparseCore 0:
  70.0 218.3 all-gather.2
where the time goes:
time: 704 us; the launch traced here: 696 us
  other arithmetic  232 us (33%)
  local copies, waits for them, and re-layouts  139 us (20%)
  waiting for transfers between devices  121 us (17%)
  matrix products  121 us (17%)
  blocking collectives  41 us (6%)
  starting transfers between devices  26.9 us (4%)
  between operations  15.1 us (2%)
    dot_general x9, matrix products, digit_products(): jnp.einsum('prk,pkc->prc', left_digits[first_digit], right_digits[second_...  121 us
    select_n x45, other arithmetic, add_mod(): return jnp.where(summed >= modulus, summed - modulus, summed)  115 us
    all_to_all x1, waiting for transfers between devices, on_device(): lax.all_to_all(forward_local(spread[0]), 'deg', split_axis=0, concat_axis...  83.5 us
    dot_general x9, local copies, waits for them, and re-layouts, digit_products(): jnp.einsum('prk,pkc->prc', left_digits[first_digit], right_digits[second_...  51.8 us
    rem x3, other arithmetic, mul_mod(): return jnp.remainder(residual, modulus).astype(first.dtype)  45.3 us
    select_n x12, other arithmetic, sub_mod(): return jnp.where(differ < 0, differ + modulus, differ)  29.9 us
    reshape x2, local copies, waits for them, and re-layouts, on_device(): piece.reshape(2 * coef_rows, inner, COLS)  27.3 us
    all_to_all x1, waiting for transfers between devices, on_device(): lax.all_to_all(left.reshape(1, coef_rows, -1), 'deg', split_axis=1, conca...  23.1 us
  transfers between devices with their start and end apart: 5, of which 3 were waited for; matrix products, arithmetic and copies ran while one was open for 26% of the time, Pallas kernels for 0%

commit v1 on v0

v1 whole, which is shorter than its diff:
```python
import jax
import jax.numpy as jnp
import numpy as np
from jax import lax
from jax.experimental import pallas as pl
from jax.experimental.pallas import tpu as pltpu
from jax.sharding import PartitionSpec as P

K = 64
COLS = 16
modulus = 7340033
generator = 3

BLOCK = 1024
POINTS = 2048
N_DEG = 16
N_ROW = 8
N_DEV = N_DEG * N_ROW
PER = POINTS // N_DEV
FACTORS = (64, 32)
AXES = ("deg", "row")
VMEM_LIMIT = 60 * 1024 * 1024

ROUND = 1.5 * 2.0**23
ROUND_8 = ROUND * 2.0**8
ROUND_16 = ROUND * 2.0**16
HIGH = 7.0 * 2.0**20


def root_powers(order):
    root = pow(generator, (modulus - 1) // order, modulus)
    values = np.ones(order, dtype=np.int64)
    for position in range(1, order):
        values[position] = values[position - 1] * root % modulus
    return values


def digit_matrix(matrix):
    columns = []
    for a in range(3):
        value = matrix * pow(2, 8 * a, modulus) % modulus
        value = np.where(value > modulus // 2, value - modulus, value)
        low = ((value + 128) & 255) - 128
        value = (value - low) >> 8
        middle = ((value + 128) & 255) - 128
        high = (value - middle) >> 8
        rows = np.concatenate([low, middle, high], axis=-2)
        columns.append(rows * 2.0 ** (-8 * a))
    return np.concatenate(columns, axis=-1).astype(np.float32)


def forward_tables():
    powers = root_powers(POINTS)
    k1, m1, m0 = np.arange(64), np.arange(32), np.arange(32)
    first = powers[(32 * m1[None, None, :] + m0[:, None, None]) * k1[None, :, None] % POINTS]
    k0 = np.arange(32)
    second = powers[64 * k0[:, None] * m0[None, :] % POINTS]
    return digit_matrix(first), digit_matrix(second)


def backward_tables():
    powers = root_powers(POINTS)
    k1, k0, m0, m1 = np.arange(64), np.arange(32), np.arange(32), np.arange(32)
    exponent = m0[None, :, None] * (64 * k0[None, None, :] + k1[:, None, None])
    first = powers[-exponent % POINTS] * pow(POINTS, modulus - 2, modulus) % modulus
    second = powers[-32 * m1[:, None] * k1[None, :] % POINTS]
    return digit_matrix(first), digit_matrix(second)


def split(value):
    high = (value + ROUND_16) - ROUND_16
    rest = value - high
    middle = (rest + ROUND_8) - ROUND_8
    return rest - middle, middle, high


def digit_rows(value):
    return jnp.concatenate([digit.astype(jnp.bfloat16) for digit in split(value)], axis=0)


def fold(sums):
    s0, s1, s2 = sums
    quotient = s2 * (65536.0 / modulus) + s1 * (256.0 / modulus)
    quotient = (quotient + ROUND) - ROUND
    return ((s2 * 65536.0 - quotient * HIGH) + s1 * 256.0) + (s0 - quotient)


def times_256(value):
    quotient = (value * (256.0 / modulus) + ROUND) - ROUND
    return (value * 256.0 - quotient * HIGH) - quotient


def matmul(first, second):
    return jnp.dot(first, second, preferred_element_type=jnp.float32)


def thirds(value):
    rows = value.shape[0] // 3
    return value[:rows], value[rows : 2 * rows], value[2 * rows :]


def forward_kernel(first_ref, second_ref, *refs):
    tiles = len(refs) // 2
    x_refs, out_ref, middle_refs = refs[:tiles], refs[tiles], refs[tiles + 1 :]

    def first_step(m0, carry):
        value = jnp.concatenate([ref[pl.ds(m0, 32, stride=32), :] for ref in x_refs], axis=1)
        value = fold(thirds(matmul(first_ref[m0], digit_rows(value))))
        for tile, ref in enumerate(middle_refs):
            ref[pl.ds(m0, 64, stride=32), :] = value[:, 128 * tile : 128 * tile + 128]
        return carry

    lax.fori_loop(0, 32, first_step, 0, unroll=2)
    second = second_ref[...]

    def second_step(k1, carry):
        rows = pl.ds(pl.multiple_of(k1 * 32, 32), 32)
        value = jnp.concatenate([ref[rows, :] for ref in middle_refs], axis=1)
        out_ref[rows, :] = fold(thirds(matmul(second, digit_rows(value))))
        return carry

    lax.fori_loop(0, 64, second_step, 0, unroll=2)


def forward(block, lanes):
    first, second = (jnp.asarray(table, dtype=jnp.bfloat16) for table in forward_tables())
    columns = block.shape[1]
    tiles = lanes // 128
    return pl.pallas_call(
        forward_kernel,
        grid=(columns // lanes,),
        in_specs=[
            pl.BlockSpec(first.shape, lambda step: (0, 0, 0)),
            pl.BlockSpec(second.shape, lambda step: (0, 0)),
        ]
        + [
            pl.BlockSpec((BLOCK, 128), lambda step, tile=tile: (0, step * tiles + tile))
            for tile in range(tiles)
        ],
        out_specs=pl.BlockSpec((POINTS, lanes), lambda step: (0, step)),
        out_shape=jax.ShapeDtypeStruct((POINTS, columns), jnp.float32),
        scratch_shapes=[pltpu.VMEM((POINTS, 128), jnp.float32)] * tiles,
        compiler_params=pltpu.CompilerParams(vmem_limit_bytes=VMEM_LIMIT),
        name="forward",
    )(first, second, *[block] * tiles)


def backward_kernel(first_ref, second_ref, x_ref, out_ref, *middle_refs):
    def first_step(k1, carry):
        halves = []
        for e in range(2):
            start = k1 * 64 + e * PER
            halves.append(
                jnp.concatenate(
                    [
                        x_ref[pl.ds(pl.multiple_of(start + 32 * part, PER), PER), :]
                        for part in range(2)
                    ],
                    axis=0,
                )
            )
        data = digit_rows(jnp.concatenate(halves, axis=1))
        value = fold(thirds(matmul(first_ref[k1], data)))
        for e, ref in enumerate(middle_refs):
            ref[pl.ds(k1, 32, stride=64), :] = value[:, e * 128 : e * 128 + 128]
        return carry

    lax.fori_loop(0, 64, first_step, 0, unroll=2)
    second = second_ref[...]

    def second_step(m0, carry):
        rows = pl.ds(pl.multiple_of(m0 * 64, 64), 64)
        value = jnp.concatenate([ref[rows, :] for ref in middle_refs], axis=1)
        value = fold(thirds(matmul(second, digit_rows(value))))
        value = jnp.where(value < 0.0, value + float(modulus), value) / float(modulus)
        for e in range(2):
            out_ref[pl.ds(e * BLOCK + m0, 32, stride=32), :] = value[:, e * 128 : (e + 1) * 128]
        return carry

    lax.fori_loop(0, 32, second_step, 0, unroll=2)


def backward(values):
    first, second = (jnp.asarray(table, dtype=jnp.bfloat16) for table in backward_tables())
    return pl.pallas_call(
        backward_kernel,
        out_shape=jax.ShapeDtypeStruct((2 * BLOCK, 128), jnp.float32),
        scratch_shapes=[pltpu.VMEM((POINTS, 128), jnp.float32)] * 2,
        compiler_params=pltpu.CompilerParams(vmem_limit_bytes=VMEM_LIMIT),
        name="backward",
    )(first, second, values)


def swap_groups(tiles):
    tiles = list(tiles)
    group = lax.broadcasted_iota(jnp.int32, tiles[0].shape, 1) // 16
    for bit in (1, 2, 4):
        keep = (group & bit) == 0
        for low in range(8):
            if low & bit:
                continue
            first, second = tiles[low], tiles[low + bit]
            tiles[low] = jnp.where(keep, first, pltpu.roll(second, 16 * bit, 1))
            tiles[low + bit] = jnp.where(keep, pltpu.roll(first, 128 - 16 * bit, 1), second)
    return tiles


def product_kernel(sign_ref, *refs):
    left_refs, right_ref, out_ref = refs[:4], refs[4], refs[5]
    right_scrs, weight_scr, left_scr, sum_scr, value_scr = refs[6:8], *refs[8:]
    lane = lax.broadcasted_iota(jnp.int32, (8, 128), 1)
    low_half = lane < 64
    sign = sign_ref[0]

    def point(k, carry):
        for half in range(2):
            tiles = [
                right_ref[pl.ds((half * 8 + d) * 8 * PER + k, 8, stride=PER), :] for d in range(8)
            ]
            for i8, tile in enumerate(swap_groups(tiles)):
                right_scrs[half][pl.ds(i8, 8, stride=8), :] = tile
        value = jnp.concatenate([scr[...] for scr in right_scrs], axis=1)
        for a in range(3):
            if a:
                value = times_256(value)
            for b, digit in enumerate(split(value)):
                digit = (digit * 2.0 ** (-8 * (a + b))).astype(jnp.bfloat16)
                weight_scr[a * 64 : a * 64 + 64, b * 256 : b * 256 + 256] = digit
                if a == 2:
                    weight_scr[192:256, b * 256 : b * 256 + 256] = digit
        for pair in range(4):
            rows = [[], []]
            for d in range(N_DEG):
                tile = left_refs[pair][pl.ds(d * 8 * PER + k, 8, stride=PER), :]
                d0, d1, d2 = split(tile)
                d0_other, d1_other = pltpu.roll(d0, 64, 1), pltpu.roll(d1, 64, 1)
                rows[0].append(
                    (jnp.where(low_half, d0, d1_other), jnp.where(low_half, d2, 0.0))
                )
                rows[1].append(
                    (jnp.where(low_half, d0_other, d1), jnp.where(low_half, 0.0, d2))
                )
            for odd in range(2):
                start = (2 * pair + odd) * 128
                for part in range(2):
                    left_scr[start : start + 128, part * 128 : part * 128 + 128] = jnp.concatenate(
                        [row[part] for row in rows[odd]], axis=0
                    ).astype(jnp.bfloat16)
        sum_scr[...] = matmul(left_scr[...], weight_scr[...])

        def one_row(r8, carry):
            base = pl.multiple_of(r8 * 128, 128)
            totals = []
            for b in range(3):
                total = None
                for group in ((0, 1, 2), (3, 4, 5), (6, 7)):
                    parts = [0.0] * 4
                    for shift in group:
                        tiles = [
                            [
                                sum_scr[
                                    pl.ds(base + (8 * high + shift) * 8, 8),
                                    b * 256 + 128 * t : b * 256 + 128 * t + 128,
                                ]
                                for t in range(2)
                            ]
                            for high in range(2)
                        ]
                        tiles = [tiles[0][0], tiles[0][1] + tiles[1][0], tiles[1][1]]
                        if shift:
                            tiles = [pltpu.roll(tile, 16 * shift, 1) for tile in tiles]
                            keep = lane >= 16 * shift
                            tiles = [
                                jnp.where(keep, tiles[0], 0.0),
                                jnp.where(keep, tiles[1], tiles[0]),
                                jnp.where(keep, tiles[2], tiles[1]),
                                jnp.where(keep, 0.0, tiles[2]),
                            ]
                        parts = [
                            part + tile for part, tile in zip(parts, tiles + [0.0] * (4 - len(tiles)))
                        ]
                    parts = [part.astype(jnp.int32) for part in parts]
                    total = parts if total is None else [x + y for x, y in zip(total, parts)]
                totals.append(total)
            before = jnp.zeros((8, 128), jnp.float32)
            for t in range(4):
                s0, s1, s2 = (total[t] for total in totals)
                quotient = (
                    s2.astype(jnp.float32) * (65536.0 / modulus)
                    + s1.astype(jnp.float32) * (256.0 / modulus)
                    + s0.astype(jnp.float32) * (1.0 / modulus)
                )
                quotient = ((quotient + ROUND) - ROUND).astype(jnp.int32)
                rest = (s2 << 16) + (s1 << 8) + s0 - quotient - ((quotient * 7) << 20)
                value = rest.astype(jnp.float32)
                shifted = pltpu.roll(value, 16, 1)
                value_scr[pl.ds(pl.multiple_of(r8 * 8, 8), 8), t * 128 : t * 128 + 128] = (
                    value + sign * jnp.where(lane < 16, before, shifted)
                )
                before = shifted
            return carry

        lax.fori_loop(0, 8, one_row, 0)
        for t in range(4):
            tiles = [value_scr[r8 * 8 : r8 * 8 + 8, t * 128 : t * 128 + 128] for r8 in range(8)]
            for g, tile in enumerate(swap_groups(tiles)):
                e = 8 * t + g
                start = (e // 2) * 8 * 2 * PER + (e % 2) * PER
                out_ref[pl.ds(start + k, 8, stride=2 * PER), :] = tile
        return carry

    lax.fori_loop(0, PER, point, 0)


def product(sign, left, right):
    return pl.pallas_call(
        product_kernel,
        grid=(1,),
        in_specs=[pl.BlockSpec(memory_space=pltpu.SMEM)]
        + [
            pl.BlockSpec((POINTS, 128), lambda step, tile=tile: (0, tile)) for tile in range(4)
        ]
        + [pl.BlockSpec((POINTS, 128), lambda step: (0, 0))],
        out_specs=pl.BlockSpec((2 * POINTS, 128), lambda step: (0, 0)),
        out_shape=jax.ShapeDtypeStruct((2 * POINTS, 128), jnp.float32),
        scratch_shapes=[
            pltpu.VMEM((64, 128), jnp.float32),
            pltpu.VMEM((64, 128), jnp.float32),
            pltpu.VMEM((256, 768), jnp.bfloat16),
            pltpu.VMEM((1024, 256), jnp.bfloat16),
            pltpu.VMEM((1024, 768), jnp.float32),
            pltpu.VMEM((64, 512), jnp.float32),
        ],
        compiler_params=pltpu.CompilerParams(vmem_limit_bytes=VMEM_LIMIT),
        name="product",
    )(sign, *[left] * 4, right)


def exchange(values, rows):
    parts = values.reshape(N_DEV, rows, values.shape[1])
    moved = lax.all_to_all(parts, AXES, split_axis=0, concat_axis=0, tiled=True)
    return moved.reshape(values.shape)


def on_device(left, right):
    mine = lax.axis_index("deg") * N_ROW + lax.axis_index("row")
    sign = (1 - 2 * ((mine // 2) % 2)).astype(jnp.float32).reshape(1)
    right_points = exchange(forward(right, 128), PER)
    left_points = exchange(forward(left, 256), PER)
    values = product(sign, left_points, right_points)
    return backward(exchange(values, 2 * PER))


def solution(mesh):
    return jax.shard_map(
        on_device,
        mesh=mesh,
        in_specs=(P("deg", "row"), P("deg", "row")),
        out_specs=P("deg", "row"),
        check_vma=False,
    )
```

time: 704 us -> 219 us (0.31); the launches traced: 696 us -> 218 us
  other arithmetic: 232 us -> 0 us
  local copies, waits for them, and re-layouts: 139 us -> 0.97 us
  matrix products: 121 us -> 0 us
  Pallas kernels: 0 us -> 107 us
  waiting for transfers between devices: 121 us -> 52.2 us
  between operations: 15.1 us -> 0.05 us
    select_n x58 -> x0, other arithmetic: 145 us -> none  [the longest x45 115 us: add_mod(): return jnp.where(summed >= modulus, summed - modulus, summed)]
    dot_general x9 -> x0, matrix products: 121 us -> none  [digit_products(): jnp.einsum('prk,pkc->prc', left_digits[first_digit], right_digits[second_...]
    pallas_call x0 -> x4, Pallas kernels: none -> 107 us  [the longest x1 53.3 us: product(): pl.pallas_call(product_kernel, grid=(1,), in_specs=[pl.BlockSpec(memory_s...]
    all_to_all x4 -> x2, waiting for transfers between devices: 121 us -> 52.2 us  [exchange(): moved = lax.all_to_all(parts, AXES, split_axis=0, concat_axis=0, tiled=True)]
    dot_general x9 -> x0, local copies, waits for them, and re-layouts: 51.8 us -> none  [digit_products(): jnp.einsum('prk,pkc->prc', left_digits[first_digit], right_digits[second_...]
    rem x3 -> x0, other arithmetic: 45.3 us -> none  [mul_mod(): return jnp.remainder(residual, modulus).astype(first.dtype)]
    reshape x5 -> x0, local copies, waits for them, and re-layouts: 30.7 us -> none  [the longest x2 27.3 us: on_device(): piece.reshape(2 * coef_rows, inner, COLS)]
    gather x4 -> x0, local copies, waits for them, and re-layouts: 23.6 us -> none  [the longest x2 11.8 us: on_device(): jnp.take(forward_table, freqs[:, None] * positions[None, :] % length)]
  transfers between devices with their start and end apart: 5 -> 2, of which waited for: 3 -> 1; matrix products, arithmetic and copies ran while one was open for 26% -> 0% of each run, Pallas kernels for 0% -> 12%
where the time goes in v1:
time: 219 us; the launch traced here: 218 us
  Pallas kernels  107 us (49%)
  waiting for transfers between devices  52.2 us (24%)
  blocking collectives  36.5 us (17%)
  starting transfers between devices  21.7 us (10%)
    pallas_call x1, Pallas kernels, product(): pl.pallas_call(product_kernel, grid=(1,), in_specs=[pl.BlockSpec(memory_s...  53.3 us
    all_to_all x2, waiting for transfers between devices, exchange(): moved = lax.all_to_all(parts, AXES, split_axis=0, concat_axis=0, tiled=True)  52.2 us
    pallas_call x2, Pallas kernels, forward(): pl.pallas_call(forward_kernel, grid=(columns // lanes,), in_specs=[pl.Blo...  38.7 us
    all_to_all x1, blocking collectives, exchange(): moved = lax.all_to_all(parts, AXES, split_axis=0, concat_axis=0, tiled=True)  36.5 us
    all_to_all x2, starting transfers between devices, exchange(): moved = lax.all_to_all(parts, AXES, split_axis=0, concat_axis=0, tiled=True)  21.7 us
    pallas_call x1, Pallas kernels, backward(): pl.pallas_call(backward_kernel, out_shape=jax.ShapeDtypeStruct((2 * BLOCK...  14.6 us
  transfers between devices with their start and end apart: 2, of which 1 were waited for; matrix products, arithmetic and copies ran while one was open for 0% of the time, Pallas kernels for 12%

profile of v1, /device:TPU:1, one launch (start us, length us, event | category | flops | bytes accessed | tf_op | source)
XLA Modules:
  0.0 218.2 jit_solution(4955118385344306307)
XLA Ops:
  0.0 11.7 %forward.3 = f32[2048,128]{1,0:T(8,128)} custom-call(bf16[32,192,96]{2,1,0:T(8,128)(2,1)} %constant.44.clone.first_ref, bf16[96,96]{1,0:T(8,128)(2,1)} %constant.45.clone.second_ref, f32[1024,128]{1,0:T(8,128)} %refs_0_.3), custom_call_target="tpu_custom_call" | custom-call | tf_op jit(solution)/shard_map/forward/pallas_call | solution.py:129
  11.7 11.5 %all-to-all-start.1 = ((f32[128,16,128]{2,1,0:T(8,128)}), f32[128,16,128]{2,1,0:T(8,128)S(1)}, u32[]{:S(2)}, u32[]{:S(2)}) async-start(f32[128,16,128]{2,1,0:T(8,128)} %bitcast.11), calls=%async_computation.1 | async-start | bytes 2097152 | tf_op jit(solution)/shard_map/all_to_all | solution.py:341
  23.2 27.1 %forward.2 = f32[2048,512]{1,0:T(8,128)} custom-call(bf16[32,192,96]{2,1,0:T(8,128)(2,1)} %constant.44.clone.first_ref, bf16[96,96]{1,0:T(8,128)(2,1)} %constant.45.clone.second_ref, f32[1024,512]{1,0:T(8,128)} %refs_1_.1, f32[1024,512]{1,0:T(8,128)} %refs_1_.1), custom_call_target="tpu_custom_call" | custom-call | tf_op jit(solution)/shard_map/forward/pallas_call | solution.py:129
  50.2 0.0 all-to-all-done.1
  50.2 0.0 copy-start
  50.2 1.0 copy-done
  51.2 10.2 %all-to-all-start = ((f32[128,16,512]{2,1,0:T(8,128)}), f32[128,16,512]{2,1,0:T(8,128)}, u32[]{:S(2)}, u32[]{:S(2)}) async-start(f32[128,16,512]{2,1,0:T(8,128)} %bitcast.7), calls=%async_computation | async-start | bytes 8388608 | tf_op jit(solution)/shard_map/all_to_all | solution.py:341
  61.5 52.2 %all-to-all-done = f32[128,16,512]{2,1,0:T(8,128)} async-done(((f32[128,16,512]{2,1,0:T(8,128)}), f32[128,16,512]{2,1,0:T(8,128)}, u32[]{:S(2)}, u32[]{:S(2)}) %all-to-all-start) | async-done | bytes 4194336 | tf_op jit(solution)/shard_map/all_to_all | solution.py:341
  113.7 53.3 %product.1 = f32[4096,128]{1,0:T(8,128)} custom-call(f32[1]{0:T(128)} %bitcast.sign_ref, f32[2048,512]{1,0:T(8,128)} %bitcast.2.refs_0_.refs_1_.refs_2_.refs_3_, f32[2048,512]{1,0:T(8,128)} %bitcast.2.refs_0_.refs_1_.refs_2_.refs_3_, f32[2048,512]{1,0:T(8,128)} %bitcast.2.refs_0_.refs_1_.refs_2_.refs_3_, f32[2048,512]{1,0:T(8,128)} %bitcast.2.refs_0_.refs_1_.refs_2_.refs_3_, ...), custom_call_target="tpu_custom_call" | custom-call | tf_op jit(solution)/shard_map/product/pallas_call | solution.py:316
  167.0 36.5 %all_to_all.15 = f32[128,32,128]{2,1,0:T(8,128)} all-to-all(f32[128,32,128]{2,1,0:T(8,128)} %bitcast.9), channel_id=1, replica_groups=mesh['deg'=16,'row'=8] {'deg','row'}, dimensions={0} | all-to-all | bytes 4194304 | tf_op jit(solution)/shard_map/all_to_all | solution.py:341
  203.6 14.6 %backward.1 = f32[2048,128]{1,0:T(8,128)} custom-call(bf16[64,96,96]{2,1,0:T(8,128)(2,1)} %constant.46.clone.first_ref, bf16[96,192]{1,0:T(8,128)(2,1)} %constant.47.clone.second_ref, f32[4096,128]{1,0:T(8,128)} %bitcast.8), custom_call_target="tpu_custom_call" | custom-call | tf_op jit(solution)/shard_map/backward/pallas_call | solution.py:185
Async XLA Ops:
  11.7 38.6 %all-to-all-start.1 = ((f32[128,16,128]{2,1,0:T(8,128)}), f32[128,16,128]{2,1,0:T(8,128)S(1)}, u32[]{:S(2)}, u32[]{:S(2)}) async-start(f32[128,16,128]{2,1,0:T(8,128)} %bitcast.11), calls=%async_computation.1 | async-start | bytes 2097152 | tf_op jit(solution)/shard_map/all_to_all | solution.py:341
  50.2 1.0 copy-start
  51.2 62.5 %all-to-all-start = ((f32[128,16,512]{2,1,0:T(8,128)}), f32[128,16,512]{2,1,0:T(8,128)}, u32[]{:S(2)}, u32[]{:S(2)}) async-start(f32[128,16,512]{2,1,0:T(8,128)} %bitcast.7), calls=%async_computation | async-start | bytes 8388608 | tf_op jit(solution)/shard_map/all_to_all | solution.py:341

commit v2 on v1

v2 whole, which is shorter than its diff:
```python
import functools

import jax
import jax.numpy as jnp
import numpy as np
from jax import lax
from jax.experimental import pallas as pl
from jax.experimental.pallas import tpu as pltpu
from jax.sharding import PartitionSpec as P

K = 64
COLS = 16
modulus = 7340033
generator = 3

BLOCK = 1024
POINTS = 2048
N_DEG = 16
N_ROW = 8
N_DEV = N_DEG * N_ROW
PER = POINTS // N_DEV
FACTORS = (64, 32)
AXES = ("deg", "row")
CHUNKS = 2
CHUNK_ROWS = 4
STEP = 2
PITCH = 40
PITCH_BACK = 72
UNROLL = 16
VMEM_LIMIT = 60 * 1024 * 1024

ROUND = 1.5 * 2.0**23
ROUND_8 = ROUND * 2.0**8
ROUND_16 = ROUND * 2.0**16
HIGH = 7.0 * 2.0**20


def root_powers(order):
    root = pow(generator, (modulus - 1) // order, modulus)
    values = np.ones(order, dtype=np.int64)
    for position in range(1, order):
        values[position] = values[position - 1] * root % modulus
    return values


def digit_matrix(matrix):
    columns = []
    for a in range(3):
        value = matrix * pow(2, 8 * a, modulus) % modulus
        value = np.where(value > modulus // 2, value - modulus, value)
        low = ((value + 128) & 255) - 128
        value = (value - low) >> 8
        middle = ((value + 128) & 255) - 128
        high = (value - middle) >> 8
        rows = np.concatenate([low, middle, high], axis=-2)
        columns.append(rows * 2.0 ** (-8 * a))
    return np.concatenate(columns, axis=-1).astype(np.float32)


def forward_tables():
    powers = root_powers(POINTS)
    k1, m1, m0 = np.arange(64), np.arange(32), np.arange(32)
    first = powers[(32 * m1[None, None, :] + m0[:, None, None]) * k1[None, :, None] % POINTS]
    k0 = np.arange(32)
    second = powers[64 * k0[:, None] * m0[None, :] % POINTS]
    return digit_matrix(first), digit_matrix(second)


def backward_tables():
    powers = root_powers(POINTS)
    k1, k0, m0, m1 = np.arange(64), np.arange(32), np.arange(32), np.arange(32)
    exponent = m0[None, :, None] * (64 * k0[None, None, :] + k1[:, None, None])
    first = powers[-exponent % POINTS] * pow(POINTS, modulus - 2, modulus) % modulus
    second = powers[-32 * m1[:, None] * k1[None, :] % POINTS]
    return digit_matrix(first), digit_matrix(second)


def split(value):
    high = (value + ROUND_16) - ROUND_16
    rest = value - high
    middle = (rest + ROUND_8) - ROUND_8
    return rest - middle, middle, high


def digit_rows(value):
    return jnp.concatenate([digit.astype(jnp.bfloat16) for digit in split(value)], axis=0)


def fold(sums):
    s0, s1, s2 = sums
    quotient = s2 * (65536.0 / modulus) + s1 * (256.0 / modulus)
    quotient = (quotient + ROUND) - ROUND
    return ((s2 * 65536.0 - quotient * HIGH) + s1 * 256.0) + (s0 - quotient)


def times_256(value):
    quotient = (value * (256.0 / modulus) + ROUND) - ROUND
    return (value * 256.0 - quotient * HIGH) - quotient


def matmul(first, second):
    return jnp.dot(first, second, preferred_element_type=jnp.float32)


def thirds(value):
    rows = value.shape[0] // 3
    return value[:rows], value[rows : 2 * rows], value[2 * rows :]


def forward_kernel(tiles, first_ref, second_ref, *refs):
    x_refs, out_ref, middle_refs = refs[:tiles], refs[tiles], refs[tiles + 1 :]

    def first_step(m0, carry):
        value = jnp.concatenate([ref[pl.ds(m0, 32, stride=32), :] for ref in x_refs], axis=1)
        value = fold(thirds(matmul(first_ref[m0], digit_rows(value))))
        for tile, ref in enumerate(middle_refs):
            ref[pl.ds(m0, 64, stride=PITCH), :] = value[:, 128 * tile : 128 * tile + 128]
        return carry

    lax.fori_loop(0, 32, first_step, 0, unroll=UNROLL)
    second = second_ref[...]

    def second_step(k1, carry):
        rows = pl.ds(pl.multiple_of(k1 * PITCH, 8), 32)
        value = jnp.concatenate([ref[rows, :] for ref in middle_refs], axis=1)
        rows = pl.ds(pl.multiple_of(k1 * 32, 32), 32)
        out_ref[rows, :] = fold(thirds(matmul(second, digit_rows(value))))
        return carry

    lax.fori_loop(0, 64, second_step, 0, unroll=UNROLL)


def forward(*columns):
    first, second = (jnp.asarray(table, dtype=jnp.bfloat16) for table in forward_tables())
    tiles = len(columns)
    return pl.pallas_call(
        functools.partial(forward_kernel, tiles),
        grid=(1,),
        in_specs=[
            pl.BlockSpec(first.shape, lambda step: (0, 0, 0)),
            pl.BlockSpec(second.shape, lambda step: (0, 0)),
        ]
        + [
            pl.BlockSpec((BLOCK, 128), lambda step, tile=tile: (0, tile)) for _, tile in columns
        ],
        out_specs=pl.BlockSpec((POINTS, tiles * 128), lambda step: (0, 0)),
        out_shape=jax.ShapeDtypeStruct((POINTS, tiles * 128), jnp.float32),
        scratch_shapes=[pltpu.VMEM((64 * PITCH, 128), jnp.float32)] * tiles,
        compiler_params=pltpu.CompilerParams(vmem_limit_bytes=VMEM_LIMIT),
        cost_estimate=pl.CostEstimate(
            flops=tiles * 3 * 10**9, bytes_accessed=tiles * 3 * 2**19, transcendentals=0
        ),
        name="forward",
    )(first, second, *[array for array, _ in columns])


def backward_kernel(first_ref, second_ref, *refs):
    x_refs, out_ref, middle_refs = refs[:CHUNKS], refs[CHUNKS], refs[CHUNKS + 1 :]
    low_half = lax.broadcasted_iota(jnp.int32, (32, 128), 1) < 64

    def first_step(k1, carry):
        rows = pl.ds(pl.multiple_of(k1 * 32, 32), 32)
        data = digit_rows(jnp.concatenate([ref[rows, :] for ref in x_refs], axis=1))
        value = fold(thirds(matmul(first_ref[k1], data)))
        for chunk, ref in enumerate(middle_refs):
            ref[pl.ds(k1, 32, stride=PITCH_BACK), :] = value[:, chunk * 128 : chunk * 128 + 128]
        return carry

    lax.fori_loop(0, 64, first_step, 0, unroll=UNROLL)
    second = second_ref[...]

    def second_step(m0, carry):
        rows = pl.ds(pl.multiple_of(m0 * PITCH_BACK, 8), 64)
        value = jnp.concatenate([ref[rows, :] for ref in middle_refs], axis=1)
        value = fold(thirds(matmul(second, digit_rows(value))))
        value = jnp.where(value < 0.0, value + float(modulus), value) / float(modulus)
        low, high = value[:, :128], value[:, 128:]
        out_ref[pl.ds(m0, 32, stride=32), :] = jnp.where(low_half, low, pltpu.roll(high, 64, 1))
        out_ref[pl.ds(BLOCK + m0, 32, stride=32), :] = jnp.where(
            low_half, pltpu.roll(low, 64, 1), high
        )
        return carry

    lax.fori_loop(0, 32, second_step, 0, unroll=UNROLL)


def backward(chunks):
    first, second = (jnp.asarray(table, dtype=jnp.bfloat16) for table in backward_tables())
    return pl.pallas_call(
        backward_kernel,
        out_shape=jax.ShapeDtypeStruct((2 * BLOCK, 128), jnp.float32),
        scratch_shapes=[pltpu.VMEM((32 * PITCH_BACK, 128), jnp.float32)] * CHUNKS,
        compiler_params=pltpu.CompilerParams(vmem_limit_bytes=VMEM_LIMIT),
        cost_estimate=pl.CostEstimate(
            flops=8 * 10**9, bytes_accessed=3 * 2**20, transcendentals=0
        ),
        name="backward",
    )(first, second, *chunks)


def exchange_bit(tiles, index_bit, group_bit):
    tiles = list(tiles)
    lane = lax.broadcasted_iota(jnp.int32, tiles[0].shape, 1)
    keep = (lane & (16 * group_bit)) == 0
    for low in range(len(tiles)):
        if low & index_bit:
            continue
        first, second = tiles[low], tiles[low + index_bit]
        tiles[low] = jnp.where(keep, first, pltpu.roll(second, 16 * group_bit, 1))
        tiles[low + index_bit] = jnp.where(
            keep, pltpu.roll(first, 128 - 16 * group_bit, 1), second
        )
    return tiles


def weights_kernel(right_ref, out_ref, *scratch):
    step = pl.program_id(0)
    for point in range(STEP):
        scrs = scratch[2 * point : 2 * point + 2]
        for half in range(2):
            tiles = [
                right_ref[pl.ds((half * 8 + d) * 8 * PER + STEP * step + point, 8, stride=PER), :]
                for d in range(8)
            ]
            for bit in (1, 2, 4):
                tiles = exchange_bit(tiles, bit, bit)
            for i8, tile in enumerate(tiles):
                scrs[half][pl.ds(i8, 8, stride=8), :] = tile
        value = jnp.concatenate([scr[...] for scr in scrs], axis=1)
        for a in range(3):
            if a:
                value = times_256(value)
            for b, digit in enumerate(split(value)):
                digit = (digit * 2.0 ** (-8 * (a + b))).astype(jnp.bfloat16)
                out_ref[point, a * 64 : a * 64 + 64, b * 256 : b * 256 + 256] = digit
                if a == 2:
                    out_ref[point, 192:256, b * 256 : b * 256 + 256] = digit


def weights(points, tile):
    return pl.pallas_call(
        weights_kernel,
        grid=(PER // STEP,),
        in_specs=[pl.BlockSpec((POINTS, 128), lambda step: (0, tile))],
        out_specs=pl.BlockSpec((STEP, 256, 768), lambda step: (step, 0, 0)),
        out_shape=jax.ShapeDtypeStruct((PER, 256, 768), jnp.bfloat16),
        scratch_shapes=[pltpu.VMEM((64, 128), jnp.float32)] * (2 * STEP),
        compiler_params=pltpu.CompilerParams(vmem_limit_bytes=VMEM_LIMIT),
        cost_estimate=pl.CostEstimate(
            flops=3 * 10**9, bytes_accessed=7 * 2**20, transcendentals=0
        ),
        name="weights",
    )(points)


def product_kernel(sign_ref, *refs):
    left_refs, weight_ref, out_ref = refs[:2], refs[2], refs[3]
    left_scrs, sum_scrs = refs[4 : 4 + STEP], refs[4 + STEP :]
    step = pl.program_id(0)
    lane = lax.broadcasted_iota(jnp.int32, (8, 128), 1)
    low_half = lane < 64
    sign = sign_ref[0]

    def prepare(point):
        for pair in range(CHUNK_ROWS // 2):
            rows = [[], []]
            for d in range(N_DEG):
                tile = left_refs[pair][
                    pl.ds(d * 8 * PER + STEP * step + point, 8, stride=PER), :
                ]
                d0, d1, d2 = split(tile)
                d0_other, d1_other = pltpu.roll(d0, 64, 1), pltpu.roll(d1, 64, 1)
                rows[0].append(
                    (jnp.where(low_half, d0, d1_other), jnp.where(low_half, d2, 0.0))
                )
                rows[1].append(
                    (jnp.where(low_half, d0_other, d1), jnp.where(low_half, 0.0, d2))
                )
            for odd in range(2):
                start = (2 * pair + odd) * 128
                for part in range(2):
                    left_scrs[point][start : start + 128, part * 128 : part * 128 + 128] = (
                        jnp.concatenate([row[part] for row in rows[odd]], axis=0).astype(
                            jnp.bfloat16
                        )
                    )

    def multiply(point):
        sum_scrs[point][...] = matmul(left_scrs[point][...], weight_ref[point])

    def shifted_sums(sum_scr, r4, b):
        total = None
        for group in ((0, 1, 2), (3, 4, 5), (6, 7)):
            parts = None
            for shift in group:
                tiles = [
                    [
                        sum_scr[
                            pl.ds(r4 * 128 + (8 * high + shift) * 8, 8),
                            b * 256 + 128 * t : b * 256 + 128 * t + 128,
                        ]
                        for t in range(2)
                    ]
                    for high in range(2)
                ]
                tiles = [tiles[0][0], tiles[0][1] + tiles[1][0], tiles[1][1]]
                if shift:
                    tiles = [pltpu.roll(tile, 16 * shift, 1) for tile in tiles]
                    keep = lane >= 16 * shift
                    tiles = [
                        jnp.where(keep, tiles[0], 0.0),
                        jnp.where(keep, tiles[1], tiles[0]),
                        jnp.where(keep, tiles[2], tiles[1]),
                        jnp.where(keep, 0.0, tiles[2]),
                    ]
                else:
                    tiles = tiles + [jnp.zeros((8, 128), jnp.float32)]
                parts = tiles if parts is None else [x + y for x, y in zip(parts, tiles)]
            parts = [part.astype(jnp.int32) for part in parts]
            total = parts if total is None else [x + y for x, y in zip(total, parts)]
        return total

    def finish(point):
        values = []
        for r4 in range(CHUNK_ROWS):
            totals = [shifted_sums(sum_scrs[point], r4, b) for b in range(3)]
            before = jnp.zeros((8, 128), jnp.float32)
            row = []
            for t in range(4):
                s0, s1, s2 = (total[t] for total in totals)
                quotient = (
                    s2.astype(jnp.float32) * (65536.0 / modulus)
                    + s1.astype(jnp.float32) * (256.0 / modulus)
                    + s0.astype(jnp.float32) * (1.0 / modulus)
                )
                quotient = ((quotient + ROUND) - ROUND).astype(jnp.int32)
                rest = (s2 << 16) + (s1 << 8) + s0 - quotient - ((quotient * 7) << 20)
                value = rest.astype(jnp.float32)
                shifted = pltpu.roll(value, 16, 1)
                row.append(value + sign * jnp.where(lane < 16, before, shifted))
                before = shifted
            values.append(row)
        for t in range(4):
            tiles = [row[t] for row in values]
            tiles = exchange_bit(tiles, 1, 1)
            tiles = exchange_bit(tiles, 1, 4)
            tiles = exchange_bit(tiles, 2, 2)
            for index, tile in enumerate(tiles):
                device = 4 * t + 2 * (index & 1) + (index >> 1)
                out_ref[pl.ds(device * 8 * PER + STEP * step + point, 8, stride=PER), :] = tile

    prepare(0)
    for point in range(STEP):
        if point + 1 < STEP:
            prepare(point + 1)
        multiply(point)
        if point:
            finish(point - 1)
    finish(STEP - 1)


def product(sign, left, right):
    return pl.pallas_call(
        product_kernel,
        grid=(PER // STEP,),
        in_specs=[pl.BlockSpec(memory_space=pltpu.SMEM)]
        + [pl.BlockSpec((POINTS, 128), lambda step, tile=tile: (0, tile)) for tile in range(2)]
        + [pl.BlockSpec((STEP, 256, 768), lambda step: (step, 0, 0))],
        out_specs=pl.BlockSpec((POINTS, 128), lambda step: (0, 0)),
        out_shape=jax.ShapeDtypeStruct((POINTS, 128), jnp.float32),
        scratch_shapes=[pltpu.VMEM((CHUNK_ROWS * 128, 256), jnp.bfloat16)] * STEP
        + [pltpu.VMEM((CHUNK_ROWS * 128, 768), jnp.float32)] * STEP,
        compiler_params=pltpu.CompilerParams(vmem_limit_bytes=VMEM_LIMIT),
        cost_estimate=pl.CostEstimate(
            flops=12 * 10**9, bytes_accessed=9 * 2**20, transcendentals=0
        ),
        name="product",
    )(sign, left, left, right)


def exchange(values):
    parts = values.reshape(N_DEV, PER, values.shape[1])
    moved = lax.all_to_all(parts, AXES, split_axis=0, concat_axis=0, tiled=True)
    return moved.reshape(values.shape)


def on_device(left, right):
    mine = lax.axis_index("deg") * N_ROW + lax.axis_index("row")
    sign = (1 - 2 * ((mine // 2) % 2)).astype(jnp.float32).reshape(1)
    first = exchange(forward((left, 0), (left, 1), (right, 0)))
    second = exchange(forward((left, 2), (left, 3)))
    factor = weights(first, 2)
    return backward([exchange(product(sign, part, factor)) for part in (first, second)])


def solution(mesh):
    return jax.shard_map(
        on_device,
        mesh=mesh,
        in_specs=(P("deg", "row"), P("deg", "row")),
        out_specs=P("deg", "row"),
        check_vma=False,
    )
```

time: 219 us -> 157 us (0.72)
  Pallas kernels: 107 us -> 55.6 us
  blocking collectives: 36.5 us -> 24.9 us
    pallas_call x3 -> x5, Pallas kernels: 92 us -> 48.7 us  [the longest x2 25.7 us: product(): pl.pallas_call(product_kernel, grid=(PER // STEP,), in_specs=[pl.BlockSpe...]
    all_to_all x1, blocking collectives: 36.5 us -> 24.9 us  [exchange(): moved = lax.all_to_all(parts, AXES, split_axis=0, concat_axis=0, tiled=True)]
    pallas_call x1, Pallas kernels: 14.6 us -> 6.95 us  [backward(): pl.pallas_call(backward_kernel, out_shape=jax.ShapeDtypeStruct((2 * BLOCK...]
    all_to_all x2 -> x3, waiting for transfers between devices: 52.2 us -> 51.7 us  [exchange(): moved = lax.all_to_all(parts, AXES, split_axis=0, concat_axis=0, tiled=True)]
    all_to_all x2 -> x3, starting transfers between devices: 21.7 us -> 22 us  [exchange(): moved = lax.all_to_all(parts, AXES, split_axis=0, concat_axis=0, tiled=True)]
  transfers between devices with their start and end apart: 2 -> 3, of which waited for: 1 -> 3; matrix products, arithmetic and copies ran while one was open for 0% -> 0% of each run, Pallas kernels for 12% -> 25%
where the time goes in v2:
time: 157 us; the launch traced here: 156 us
  Pallas kernels  55.6 us (35%)
  waiting for transfers between devices  51.7 us (33%)
  blocking collectives  24.9 us (16%)
  starting transfers between devices  22 us (14%)
  local copies, waits for them, and re-layouts  1.7 us (1%)
    all_to_all x3, waiting for transfers between devices, exchange(): moved = lax.all_to_all(parts, AXES, split_axis=0, concat_axis=0, tiled=True)  51.7 us
    pallas_call x2, Pallas kernels, product(): pl.pallas_call(product_kernel, grid=(PER // STEP,), in_specs=[pl.BlockSpe...  25.7 us
    all_to_all x1, blocking collectives, exchange(): moved = lax.all_to_all(parts, AXES, split_axis=0, concat_axis=0, tiled=True)  24.9 us
    all_to_all x3, starting transfers between devices, exchange(): moved = lax.all_to_all(parts, AXES, split_axis=0, concat_axis=0, tiled=True)  22 us
    pallas_call x2, Pallas kernels, forward(): pl.pallas_call(functools.partial(forward_kernel, tiles), grid=(1,), in_sp...  15.9 us
    pallas_call x1, Pallas kernels, weights(): pl.pallas_call(weights_kernel, grid=(PER // STEP,), in_specs=[pl.BlockSpe...  7.11 us
    pallas_call x1, Pallas kernels, backward(): pl.pallas_call(backward_kernel, out_shape=jax.ShapeDtypeStruct((2 * BLOCK...  6.95 us
  transfers between devices with their start and end apart: 3, of which 3 were waited for; matrix products, arithmetic and copies ran while one was open for 0% of the time, Pallas kernels for 25%

profile of v2, /device:TPU:1, one launch (start us, length us, event | category | flops | bytes accessed | tf_op | source)
XLA Modules:
  0.0 156.1 jit_solution(18430274322217812849)
XLA Ops:
  0.0 9.2 %forward.2 = f32[2048,384]{1,0:T(8,128)} custom-call(bf16[32,192,96]{2,1,0:T(8,128)(2,1)} %constant.44.clone.first_ref, bf16[96,96]{1,0:T(8,128)(2,1)} %constant.45.clone.second_ref, f32[1024,512]{1,0:T(8,128)} %refs_1_.3, f32[1024,512]{1,0:T(8,128)} %refs_1_.3, f32[1024,128]{1,0:T(8,128)} %refs_2_.1), custom_call_target="tpu_custom_call" | custom-call | flops 8999999488 | bytes 4718592 | tf_op jit(solution)/shard_map/forward/pallas_call | solution.py:136
  9.2 11.5 %all-to-all-start = ((f32[128,16,384]{2,1,0:T(8,128)}), f32[128,16,384]{2,1,0:T(8,128)S(1)}, u32[]{:S(2)}, u32[]{:S(2)}) async-start(f32[128,16,384]{2,1,0:T(8,128)} %bitcast.12), calls=%async_computation | async-start | bytes 6291456 | tf_op jit(solution)/shard_map/all_to_all | solution.py:383
  20.7 6.7 %forward.3 = f32[2048,256]{1,0:T(8,128)} custom-call(bf16[32,192,96]{2,1,0:T(8,128)(2,1)} %constant.44.clone.first_ref, bf16[96,96]{1,0:T(8,128)(2,1)} %constant.45.clone.second_ref, f32[1024,512]{1,0:T(8,128)} %refs_1_.3, f32[1024,512]{1,0:T(8,128)} %refs_1_.3), custom_call_target="tpu_custom_call" | custom-call | flops 6000000000 | bytes 3145728 | tf_op jit(solution)/shard_map/forward/pallas_call | solution.py:136
  27.4 34.8 %all-to-all-done = f32[128,16,384]{2,1,0:T(8,128)S(1)} async-done(((f32[128,16,384]{2,1,0:T(8,128)}), f32[128,16,384]{2,1,0:T(8,128)S(1)}, u32[]{:S(2)}, u32[]{:S(2)}) %all-to-all-start) | async-done | bytes 3145760 | tf_op jit(solution)/shard_map/all_to_all | solution.py:383
  62.2 0.0 copy-start
  62.2 1.7 %copy-done = f32[128,16,384]{2,1,0:T(8,128)} copy-done((f32[128,16,384]{2,1,0:T(8,128)}, f32[128,16,384]{2,1,0:T(8,128)S(1)}, u32[]{:S(2)}) %copy-start) | copy-done | bytes 3145752
  63.9 5.9 %all-to-all-start.2 = ((f32[128,16,256]{2,1,0:T(8,128)}), f32[128,16,256]{2,1,0:T(8,128)}, u32[]{:S(2)}, u32[]{:S(2)}) async-start(f32[128,16,256]{2,1,0:T(8,128)} %bitcast.13), calls=%async_computation.2 | async-start | bytes 4194304 | tf_op jit(solution)/shard_map/all_to_all | solution.py:383
  69.8 7.1 %weights.1.refs_2_ = bf16[16,256,768]{2,1,0:T(8,128)(2,1)} custom-call(f32[2048,384]{1,0:T(8,128)} %bitcast.9), custom_call_target="tpu_custom_call" | custom-call | flops 3000000000 | bytes 7340032 | tf_op jit(solution)/shard_map/weights/pallas_call | solution.py:241
  76.9 12.8 %product.2 = f32[2048,128]{1,0:T(8,128)} custom-call(f32[1]{0:T(128)} %bitcast.sign_ref, f32[2048,384]{1,0:T(8,128)} %bitcast.10, f32[2048,384]{1,0:T(8,128)} %bitcast.11, bf16[16,256,768]{2,1,0:T(8,128)(2,1)} %weights.1.refs_2_), custom_call_target="tpu_custom_call" | custom-call | flops 12000000000 | bytes 9437184 | tf_op jit(solution)/shard_map/product/pallas_call | solution.py:363
  89.7 10.3 %all-to-all-done.2 = f32[128,16,256]{2,1,0:T(8,128)} async-done(((f32[128,16,256]{2,1,0:T(8,128)}), f32[128,16,256]{2,1,0:T(8,128)}, u32[]{:S(2)}, u32[]{:S(2)}) %all-to-all-start.2) | async-done | bytes 2097184 | tf_op jit(solution)/shard_map/all_to_all | solution.py:383
  100.0 4.6 %all-to-all-start.1 = ((f32[128,16,128]{2,1,0:T(8,128)}), f32[128,16,128]{2,1,0:T(8,128)S(1)}, u32[]{:S(2)}, u32[]{:S(2)}) async-start(f32[128,16,128]{2,1,0:T(8,128)} %bitcast.15), calls=%async_computation.1 | async-start | bytes 2097152 | tf_op jit(solution)/shard_map/all_to_all | solution.py:383
  104.7 12.9 %product.3 = f32[2048,128]{1,0:T(8,128)} custom-call(f32[1]{0:T(128)} %bitcast.sign_ref, f32[2048,256]{1,0:T(8,128)} %bitcast.6.refs_0_.refs_1_, f32[2048,256]{1,0:T(8,128)} %bitcast.6.refs_0_.refs_1_, bf16[16,256,768]{2,1,0:T(8,128)(2,1)} %weights.1.refs_2_), custom_call_target="tpu_custom_call" | custom-call | flops 12000000000 | bytes 9437184 | tf_op jit(solution)/shard_map/product/pallas_call | solution.py:363
  117.5 6.6 %all-to-all-done.1 = f32[128,16,128]{2,1,0:T(8,128)S(1)} async-done(((f32[128,16,128]{2,1,0:T(8,128)}), f32[128,16,128]{2,1,0:T(8,128)S(1)}, u32[]{:S(2)}, u32[]{:S(2)}) %all-to-all-start.1) | async-done | bytes 1048608 | tf_op jit(solution)/shard_map/all_to_all | solution.py:383
  124.2 0.0 copy-start.1
  124.2 24.9 %all_to_all.20 = f32[128,16,128]{2,1,0:T(8,128)} all-to-all(f32[128,16,128]{2,1,0:T(8,128)} %bitcast.16), channel_id=1, replica_groups=mesh['deg'=16,'row'=8] {'deg','row'}, dimensions={0} | all-to-all | bytes 2097152 | tf_op jit(solution)/shard_map/all_to_all | solution.py:383
  149.1 0.0 copy-done.1
  149.1 6.9 %backward.1 = f32[2048,128]{1,0:T(8,128)} custom-call(bf16[64,96,96]{2,1,0:T(8,128)(2,1)} %constant.46.clone.first_ref, bf16[96,192]{1,0:T(8,128)(2,1)} %constant.47.clone.second_ref, f32[2048,128]{1,0:T(8,128)} %bitcast.14, f32[2048,128]{1,0:T(8,128)} %bitcast.17), custom_call_target="tpu_custom_call" | custom-call | flops 8000000000 | bytes 3145728 | tf_op jit(solution)/shard_map/backward/pallas_call | solution.py:189
Async XLA Ops:
  9.2 53.0 %all-to-all-start = ((f32[128,16,384]{2,1,0:T(8,128)}), f32[128,16,384]{2,1,0:T(8,128)S(1)}, u32[]{:S(2)}, u32[]{:S(2)}) async-start(f32[128,16,384]{2,1,0:T(8,128)} %bitcast.12), calls=%async_computation | async-start | bytes 6291456 | tf_op jit(solution)/shard_map/all_to_all | solution.py:383
  62.2 1.7 %copy-start = (f32[128,16,384]{2,1,0:T(8,128)}, f32[128,16,384]{2,1,0:T(8,128)S(1)}, u32[]{:S(2)}) copy-start(f32[128,16,384]{2,1,0:T(8,128)S(1)} %all-to-all-done) | copy-start | bytes 9437188
  63.9 36.1 %all-to-all-start.2 = ((f32[128,16,256]{2,1,0:T(8,128)}), f32[128,16,256]{2,1,0:T(8,128)}, u32[]{:S(2)}, u32[]{:S(2)}) async-start(f32[128,16,256]{2,1,0:T(8,128)} %bitcast.13), calls=%async_computation.2 | async-start | bytes 4194304 | tf_op jit(solution)/shard_map/all_to_all | solution.py:383
  100.0 24.2 %all-to-all-start.1 = ((f32[128,16,128]{2,1,0:T(8,128)}), f32[128,16,128]{2,1,0:T(8,128)S(1)}, u32[]{:S(2)}, u32[]{:S(2)}) async-start(f32[128,16,128]{2,1,0:T(8,128)} %bitcast.15), calls=%async_computation.1 | async-start | bytes 2097152 | tf_op jit(solution)/shard_map/all_to_all | solution.py:383
  124.2 24.9 %copy-start.1 = (f32[128,16,128]{2,1,0:T(8,128)}, f32[128,16,128]{2,1,0:T(8,128)S(1)}, u32[]{:S(2)}) copy-start(f32[128,16,128]{2,1,0:T(8,128)S(1)} %all-to-all-done.1) | copy-start | bytes 3145732

commit v3 on v2

--- a/solution.py
+++ b/solution.py
@@ -27,7 +27,6 @@
 PITCH = 40
 PITCH_BACK = 72
 UNROLL = 16
-VMEM_LIMIT = 60 * 1024 * 1024
 
 ROUND = 1.5 * 2.0**23
 ROUND_8 = ROUND * 2.0**8
@@ -107,17 +106,49 @@
     return value[:rows], value[rows : 2 * rows], value[2 * rows :]
 
 
-def forward_kernel(tiles, first_ref, second_ref, *refs):
-    x_refs, out_ref, middle_refs = refs[:tiles], refs[tiles], refs[tiles + 1 :]
+def in_parts(source, target, sems, first_sem, parts):
+    rows = source.shape[0] // parts
+    return [
+        pltpu.make_async_copy(
+            source.at[pl.ds(part * rows, rows)],
+            target.at[pl.ds(part * rows, rows)],
+            sems.at[first_sem + part],
+        )
+        for part in range(parts)
+    ]
+
+
+def forward_kernel(columns, first_hbm, second_hbm, *refs):
+    tiles = len(columns)
+    x_hbms, out_hbm, first_ref, second_ref, out_ref = refs[:tiles], *refs[tiles : tiles + 4]
+    x_refs, middle_refs = refs[tiles + 4 : 2 * tiles + 4], refs[2 * tiles + 4 : 3 * tiles + 4]
+    sems = refs[-1]
+    x_copies = [
+        pltpu.make_async_copy(
+            x_hbm.at[:, :, pl.ds(tile * 128, 128)], x_ref.at[:, pl.ds(0, 32), :], sems.at[index]
+        )
+        for index, (x_hbm, x_ref, tile) in enumerate(zip(x_hbms, x_refs, columns))
+    ]
+    first_copies = in_parts(first_hbm, first_ref, sems, tiles, 2)
+    second_copy = pltpu.make_async_copy(second_hbm, second_ref, sems.at[tiles + 2])
+    out_copies = in_parts(out_ref, out_hbm, sems, tiles + 3, 4)
+    for copy in x_copies + first_copies + [second_copy]:
+        copy.start()
+    for copy in x_copies:
+        copy.wait()
+    x_refs = [ref.reshape(32 * PITCH, 128) for ref in x_refs]
 
     def first_step(m0, carry):
-        value = jnp.concatenate([ref[pl.ds(m0, 32, stride=32), :] for ref in x_refs], axis=1)
+        value = jnp.concatenate([ref[pl.ds(m0, 32, stride=PITCH), :] for ref in x_refs], axis=1)
         value = fold(thirds(matmul(first_ref[m0], digit_rows(value))))
         for tile, ref in enumerate(middle_refs):
             ref[pl.ds(m0, 64, stride=PITCH), :] = value[:, 128 * tile : 128 * tile + 128]
         return carry
 
-    lax.fori_loop(0, 32, first_step, 0, unroll=UNROLL)
+    for part in range(2):
+        first_copies[part].wait()
+        lax.fori_loop(part * 16, part * 16 + 16, first_step, 0, unroll=UNROLL)
+    second_copy.wait()
     second = second_ref[...]
 
     def second_step(k1, carry):
@@ -127,43 +158,49 @@
         out_ref[rows, :] = fold(thirds(matmul(second, digit_rows(value))))
         return carry
 
-    lax.fori_loop(0, 64, second_step, 0, unroll=UNROLL)
+    for part in range(4):
+        lax.fori_loop(part * 16, part * 16 + 16, second_step, 0, unroll=UNROLL)
+        out_copies[part].start()
+    for copy in out_copies:
+        copy.wait()
+
+
+ANYWHERE = pl.BlockSpec(memory_space=pl.ANY)
 
 
 def forward(*columns):
     first, second = (jnp.asarray(table, dtype=jnp.bfloat16) for table in forward_tables())
     tiles = len(columns)
     return pl.pallas_call(
-        functools.partial(forward_kernel, tiles),
-        grid=(1,),
-        in_specs=[
-            pl.BlockSpec(first.shape, lambda step: (0, 0, 0)),
-            pl.BlockSpec(second.shape, lambda step: (0, 0)),
+        functools.partial(forward_kernel, [tile for _, tile in columns]),
+        in_specs=[ANYWHERE] * (2 + tiles),
+        out_specs=ANYWHERE,
+        out_shape=jax.ShapeDtypeStruct((POINTS, tiles * 128), jnp.float32),
+        scratch_shapes=[
+            pltpu.VMEM(first.shape, jnp.bfloat16),
+            pltpu.VMEM(second.shape, jnp.bfloat16),
+            pltpu.VMEM((POINTS, tiles * 128), jnp.float32),
         ]
-        + [
-            pl.BlockSpec((BLOCK, 128), lambda step, tile=tile: (0, tile)) for _, tile in columns
-        ],
-        out_specs=pl.BlockSpec((POINTS, tiles * 128), lambda step: (0, 0)),
-        out_shape=jax.ShapeDtypeStruct((POINTS, tiles * 128), jnp.float32),
-        scratch_shapes=[pltpu.VMEM((64 * PITCH, 128), jnp.float32)] * tiles,
-        compiler_params=pltpu.CompilerParams(vmem_limit_bytes=VMEM_LIMIT),
+        + [pltpu.VMEM((32, PITCH, 128), jnp.float32)] * tiles
+        + [pltpu.VMEM((64 * PITCH, 128), jnp.float32)] * tiles
+        + [pltpu.SemaphoreType.DMA((tiles + 7,))],
+        compiler_params=pltpu.CompilerParams(vmem_limit_bytes=60 * 2**20),
         cost_estimate=pl.CostEstimate(
             flops=tiles * 3 * 10**9, bytes_accessed=tiles * 3 * 2**19, transcendentals=0
         ),
         name="forward",
-    )(first, second, *[array for array, _ in columns])
-
-
-def backward_kernel(first_ref, second_ref, *refs):
-    x_refs, out_ref, middle_refs = refs[:CHUNKS], refs[CHUNKS], refs[CHUNKS + 1 :]
+    )(first, second, *[array.reshape(32, 32, -1) for array, _ in columns])
+
+
+def backward_kernel(chunk, first_ref, second_ref, x_ref, *refs):
+    before_ref = refs[0] if chunk else None
+    out_ref, middle_ref = refs[-2:]
     low_half = lax.broadcasted_iota(jnp.int32, (32, 128), 1) < 64
 
     def first_step(k1, carry):
         rows = pl.ds(pl.multiple_of(k1 * 32, 32), 32)
-        data = digit_rows(jnp.concatenate([ref[rows, :] for ref in x_refs], axis=1))
-        value = fold(thirds(matmul(first_ref[k1], data)))
-        for chunk, ref in enumerate(middle_refs):
-            ref[pl.ds(k1, 32, stride=PITCH_BACK), :] = value[:, chunk * 128 : chunk * 128 + 128]
+        value = fold(thirds(matmul(first_ref[k1], digit_rows(x_ref[rows, :]))))
+        middle_ref[pl.ds(k1, 32, stride=PITCH_BACK), :] = value
         return carry
 
     lax.fori_loop(0, 64, first_step, 0, unroll=UNROLL)
@@ -171,31 +208,32 @@
 
     def second_step(m0, carry):
         rows = pl.ds(pl.multiple_of(m0 * PITCH_BACK, 8), 64)
-        value = jnp.concatenate([ref[rows, :] for ref in middle_refs], axis=1)
-        value = fold(thirds(matmul(second, digit_rows(value))))
+        value = fold(thirds(matmul(second, digit_rows(middle_ref[rows, :]))))
         value = jnp.where(value < 0.0, value + float(modulus), value) / float(modulus)
-        low, high = value[:, :128], value[:, 128:]
-        out_ref[pl.ds(m0, 32, stride=32), :] = jnp.where(low_half, low, pltpu.roll(high, 64, 1))
-        out_ref[pl.ds(BLOCK + m0, 32, stride=32), :] = jnp.where(
-            low_half, pltpu.roll(low, 64, 1), high
-        )
+        other = pltpu.roll(value, 64, 1)
+        for e in range(2):
+            place = pl.ds(e * BLOCK + m0, 32, stride=32)
+            mine = value if e == chunk else other
+            if chunk:
+                mine = jnp.where(low_half, before_ref[place, :], mine)
+            out_ref[place, :] = mine
         return carry
 
     lax.fori_loop(0, 32, second_step, 0, unroll=UNROLL)
 
 
-def backward(chunks):
+def backward(values, chunk, before):
     first, second = (jnp.asarray(table, dtype=jnp.bfloat16) for table in backward_tables())
     return pl.pallas_call(
-        backward_kernel,
+        functools.partial(backward_kernel, chunk),
         out_shape=jax.ShapeDtypeStruct((2 * BLOCK, 128), jnp.float32),
-        scratch_shapes=[pltpu.VMEM((32 * PITCH_BACK, 128), jnp.float32)] * CHUNKS,
-        compiler_params=pltpu.CompilerParams(vmem_limit_bytes=VMEM_LIMIT),
+        scratch_shapes=[pltpu.VMEM((32 * PITCH_BACK, 128), jnp.float32)],
+        compiler_params=pltpu.CompilerParams(vmem_limit_bytes=32 * 2**20),
         cost_estimate=pl.CostEstimate(
-            flops=8 * 10**9, bytes_accessed=3 * 2**20, transcendentals=0
+            flops=5 * 10**9, bytes_accessed=3 * 2**20, transcendentals=0
         ),
         name="backward",
-    )(first, second, *chunks)
+    )(first, second, values, *before)
 
 
 def exchange_bit(tiles, index_bit, group_bit):
@@ -245,7 +283,7 @@
         out_specs=pl.BlockSpec((STEP, 256, 768), lambda step: (step, 0, 0)),
         out_shape=jax.ShapeDtypeStruct((PER, 256, 768), jnp.bfloat16),
         scratch_shapes=[pltpu.VMEM((64, 128), jnp.float32)] * (2 * STEP),
-        compiler_params=pltpu.CompilerParams(vmem_limit_bytes=VMEM_LIMIT),
+        compiler_params=pltpu.CompilerParams(vmem_limit_bytes=32 * 2**20),
         cost_estimate=pl.CostEstimate(
             flops=3 * 10**9, bytes_accessed=7 * 2**20, transcendentals=0
         ),
@@ -370,7 +408,7 @@
         out_shape=jax.ShapeDtypeStruct((POINTS, 128), jnp.float32),
         scratch_shapes=[pltpu.VMEM((CHUNK_ROWS * 128, 256), jnp.bfloat16)] * STEP
         + [pltpu.VMEM((CHUNK_ROWS * 128, 768), jnp.float32)] * STEP,
-        compiler_params=pltpu.CompilerParams(vmem_limit_bytes=VMEM_LIMIT),
+        compiler_params=pltpu.CompilerParams(vmem_limit_bytes=60 * 2**20),
         cost_estimate=pl.CostEstimate(
             flops=12 * 10**9, bytes_accessed=9 * 2**20, transcendentals=0
         ),
@@ -390,7 +428,10 @@
     first = exchange(forward((left, 0), (left, 1), (right, 0)))
     second = exchange(forward((left, 2), (left, 3)))
     factor = weights(first, 2)
-    return backward([exchange(product(sign, part, factor)) for part in (first, second)])
+    result = []
+    for chunk, part in enumerate((first, second)):
+        result = [backward(exchange(product(sign, part, factor)), chunk, result)]
+    return result[0]
 
 
 def solution(mesh):

time: 157 us -> 151 us (0.962)
  blocking collectives: 24.9 us -> 0 us
  waiting for transfers between devices: 51.7 us -> 68.9 us
  Pallas kernels: 55.6 us -> 49.3 us
  starting transfers between devices: 22 us -> 26.6 us
  local copies, waits for them, and re-layouts: 1.7 us -> 5.46 us
    all_to_all x1 -> x0, blocking collectives: 24.9 us -> none  [exchange(): moved = lax.all_to_all(parts, AXES, split_axis=0, concat_axis=0, tiled=True)]
    all_to_all x3 -> x4, waiting for transfers between devices: 51.7 us -> 68.9 us  [exchange(): moved = lax.all_to_all(parts, AXES, split_axis=0, concat_axis=0, tiled=True)]
    all_to_all x3 -> x4, starting transfers between devices: 22 us -> 26.6 us  [exchange(): moved = lax.all_to_all(parts, AXES, split_axis=0, concat_axis=0, tiled=True)]
    unnamed x4 -> x10, local copies, waits for them, and re-layouts: 1.7 us -> 5.46 us
    pallas_call x1, Pallas kernels: 7.11 us -> 3.81 us  [weights(): pl.pallas_call(weights_kernel, grid=(PER // STEP,), in_specs=[pl.BlockSpe...]
    pallas_call x3 -> x4, Pallas kernels: 22.8 us -> 19.8 us  [the longest x2 13.3 us: forward(): pl.pallas_call(functools.partial(forward_kernel, [tile for _, tile in col...]
  transfers between devices with their start and end apart: 3 -> 4, of which waited for: 3 -> 4; matrix products, arithmetic and copies ran while one was open for 0% -> 0% of each run, Pallas kernels for 25% -> 25%
where the time goes in v3:
time: 151 us; the launch traced here: 150 us
  waiting for transfers between devices  68.9 us (46%)
  Pallas kernels  49.3 us (33%)
  starting transfers between devices  26.6 us (18%)
  local copies, waits for them, and re-layouts  5.46 us (4%)
    all_to_all x4, waiting for transfers between devices, exchange(): moved = lax.all_to_all(parts, AXES, split_axis=0, concat_axis=0, tiled=True)  68.9 us
    all_to_all x4, starting transfers between devices, exchange(): moved = lax.all_to_all(parts, AXES, split_axis=0, concat_axis=0, tiled=True)  26.6 us
    pallas_call x2, Pallas kernels, product(): pl.pallas_call(product_kernel, grid=(PER // STEP,), in_specs=[pl.BlockSpe...  25.7 us
    pallas_call x2, Pallas kernels, forward(): pl.pallas_call(functools.partial(forward_kernel, [tile for _, tile in col...  13.3 us
    pallas_call x2, Pallas kernels, backward(): pl.pallas_call(functools.partial(backward_kernel, chunk), out_shape=jax.S...  6.51 us
    unnamed x10, local copies, waits for them, and re-layouts  5.46 us
    pallas_call x1, Pallas kernels, weights(): pl.pallas_call(weights_kernel, grid=(PER // STEP,), in_specs=[pl.BlockSpe...  3.81 us
  transfers between devices with their start and end apart: 4, of which 4 were waited for; matrix products, arithmetic and copies ran while one was open for 0% of the time, Pallas kernels for 25%

profile of v3, /device:TPU:1, one launch (start us, length us, event | category | flops | bytes accessed | tf_op | source)
XLA Modules:
  0.0 150.3 jit_solution(14061168089213177558)
XLA Ops:
  0.0 7.5 %forward.3 = f32[2048,384]{1,0:T(8,128)} custom-call(bf16[32,192,96]{2,1,0:T(8,128)(2,1)} %constant.44.clone.first_hbm, bf16[96,96]{1,0:T(8,128)(2,1)} %constant.45.clone.second_hbm, f32[32,32,512]{2,1,0:T(8,128)} %bitcast.20, f32[32,32,512]{2,1,0:T(8,128)} %bitcast.21, f32[32,32,128]{2,1,0:T(8,128)} %bitcast.24), custom_call_target="tpu_custom_call" | custom-call | flops 8999999488 | bytes 4718592 | tf_op jit(solution)/shard_map/forward/pallas_call | solution.py:174
  7.5 11.5 %all-to-all-start.1 = ((f32[128,16,384]{2,1,0:T(8,128)}), f32[128,16,384]{2,1,0:T(8,128)S(1)}, u32[]{:S(2)}, u32[]{:S(2)}) async-start(f32[128,16,384]{2,1,0:T(8,128)} %bitcast.16), calls=%async_computation.1 | async-start | bytes 6291456 | tf_op jit(solution)/shard_map/all_to_all | solution.py:421
  19.0 5.8 %forward.2 = f32[2048,256]{1,0:T(8,128)} custom-call(bf16[32,192,96]{2,1,0:T(8,128)(2,1)} %constant.44.clone.first_hbm, bf16[96,96]{1,0:T(8,128)(2,1)} %constant.45.clone.second_hbm, f32[32,32,512]{2,1,0:T(8,128)} %bitcast.22, f32[32,32,512]{2,1,0:T(8,128)} %bitcast.23), custom_call_target="tpu_custom_call" | custom-call | flops 6000000000 | bytes 3145728 | tf_op jit(solution)/shard_map/forward/pallas_call | solution.py:174
  24.8 35.7 %all-to-all-done.1 = f32[128,16,384]{2,1,0:T(8,128)S(1)} async-done(((f32[128,16,384]{2,1,0:T(8,128)}), f32[128,16,384]{2,1,0:T(8,128)S(1)}, u32[]{:S(2)}, u32[]{:S(2)}) %all-to-all-start.1) | async-done | bytes 3145760 | tf_op jit(solution)/shard_map/all_to_all | solution.py:421
  60.5 0.0 copy-start
  60.5 5.9 %all-to-all-start = ((f32[128,16,256]{2,1,0:T(8,128)}), f32[128,16,256]{2,1,0:T(8,128)}, u32[]{:S(2)}, u32[]{:S(2)}) async-start(f32[128,16,256]{2,1,0:T(8,128)} %bitcast.17), calls=%async_computation | async-start | bytes 4194304 | tf_op jit(solution)/shard_map/all_to_all | solution.py:421
  66.5 0.0 copy-done
  66.5 3.8 %weights.1.refs_2_ = bf16[16,256,768]{2,1,0:T(8,128)(2,1)S(1)} custom-call(f32[2048,384]{1,0:T(8,128)S(1)} %bitcast.11), custom_call_target="tpu_custom_call" | custom-call | flops 3000000000 | bytes 7340032 | tf_op jit(solution)/shard_map/weights/pallas_call | solution.py:279
  70.3 0.0 copy-start.4
  70.3 2.6 %copy-done.4 = bf16[16,256,768]{2,1,0:T(8,128)(2,1)} copy-done((bf16[16,256,768]{2,1,0:T(8,128)(2,1)}, bf16[16,256,768]{2,1,0:T(8,128)(2,1)S(1)}, u32[]{:S(2)}) %copy-start.4) | copy-done | bytes 6291480
  73.0 12.8 %product.3 = f32[2048,128]{1,0:T(8,128)} custom-call(f32[1]{0:T(128)} %bitcast.sign_ref, f32[2048,384]{1,0:T(8,128)} %bitcast.12, f32[2048,384]{1,0:T(8,128)} %bitcast.13, bf16[16,256,768]{2,1,0:T(8,128)(2,1)} %copy-done.4), custom_call_target="tpu_custom_call" | custom-call | flops 12000000000 | bytes 9437184 | tf_op jit(solution)/shard_map/product/pallas_call | solution.py:401
  85.8 10.9 %all-to-all-done = f32[128,16,256]{2,1,0:T(8,128)} async-done(((f32[128,16,256]{2,1,0:T(8,128)}), f32[128,16,256]{2,1,0:T(8,128)}, u32[]{:S(2)}, u32[]{:S(2)}) %all-to-all-start) | async-done | bytes 2097184 | tf_op jit(solution)/shard_map/all_to_all | solution.py:421
  96.7 4.7 %all-to-all-start.3 = ((f32[128,16,128]{2,1,0:T(8,128)}), f32[128,16,128]{2,1,0:T(8,128)S(1)}, u32[]{:S(2)}, u32[]{:S(2)}) async-start(f32[128,16,128]{2,1,0:T(8,128)} %bitcast.18), calls=%async_computation.3 | async-start | bytes 2097152 | tf_op jit(solution)/shard_map/all_to_all | solution.py:421
  101.3 12.8 %product.2 = f32[2048,128]{1,0:T(8,128)} custom-call(f32[1]{0:T(128)} %bitcast.sign_ref, f32[2048,256]{1,0:T(8,128)} %bitcast.3.refs_0_.refs_1_, f32[2048,256]{1,0:T(8,128)} %bitcast.3.refs_0_.refs_1_, bf16[16,256,768]{2,1,0:T(8,128)(2,1)} %copy-done.4), custom_call_target="tpu_custom_call" | custom-call | flops 12000000000 | bytes 9437184 | tf_op jit(solution)/shard_map/product/pallas_call | solution.py:401
  114.2 0.0 copy-start.3
  114.2 6.7 %all-to-all-done.3 = f32[128,16,128]{2,1,0:T(8,128)S(1)} async-done(((f32[128,16,128]{2,1,0:T(8,128)}), f32[128,16,128]{2,1,0:T(8,128)S(1)}, u32[]{:S(2)}, u32[]{:S(2)}) %all-to-all-start.3) | async-done | bytes 1048608 | tf_op jit(solution)/shard_map/all_to_all | solution.py:421
  120.8 4.5 %all-to-all-start.2 = ((f32[128,16,128]{2,1,0:T(8,128)}), f32[128,16,128]{2,1,0:T(8,128)S(1)}, u32[]{:S(2)}, u32[]{:S(2)}) async-start(f32[128,16,128]{2,1,0:T(8,128)} %bitcast.19), calls=%async_computation.2 | async-start | bytes 2097152 | tf_op jit(solution)/shard_map/all_to_all | solution.py:421
  125.4 0.0 copy-done.3
  125.4 0.0 copy-start.1
  125.4 1.4 copy-done.1
  126.8 2.5 %backward.2.refs_0_ = f32[2048,128]{1,0:T(8,128)S(1)} custom-call(bf16[64,96,96]{2,1,0:T(8,128)(2,1)S(1)} %copy-done.1, bf16[96,192]{1,0:T(8,128)(2,1)S(1)} %copy-done.3, f32[2048,128]{1,0:T(8,128)S(1)} %bitcast.14), custom_call_target="tpu_custom_call" | custom-call | flops 5000000000 | bytes 3145728 | tf_op jit(solution)/shard_map/backward/pallas_call | solution.py:227
  129.2 15.6 %all-to-all-done.2 = f32[128,16,128]{2,1,0:T(8,128)S(1)} async-done(((f32[128,16,128]{2,1,0:T(8,128)}), f32[128,16,128]{2,1,0:T(8,128)S(1)}, u32[]{:S(2)}, u32[]{:S(2)}) %all-to-all-start.2) | async-done | bytes 1048608 | tf_op jit(solution)/shard_map/all_to_all | solution.py:421
  144.9 0.0 copy-start.2
  144.9 1.4 copy-done.2
  146.3 4.0 %backward.3 = f32[2048,128]{1,0:T(8,128)} custom-call(bf16[64,96,96]{2,1,0:T(8,128)(2,1)S(1)} %copy-done.2, bf16[96,192]{1,0:T(8,128)(2,1)S(1)} %copy-done.3, f32[2048,128]{1,0:T(8,128)S(1)} %bitcast.15, f32[2048,128]{1,0:T(8,128)S(1)} %backward.2.refs_0_), custom_call_target="tpu_custom_call" | custom-call | flops 5000000000 | bytes 3145728 | tf_op jit(solution)/shard_map/backward/pallas_call | solution.py:227
Async XLA Ops:
  7.5 53.0 %all-to-all-start.1 = ((f32[128,16,384]{2,1,0:T(8,128)}), f32[128,16,384]{2,1,0:T(8,128)S(1)}, u32[]{:S(2)}, u32[]{:S(2)}) async-start(f32[128,16,384]{2,1,0:T(8,128)} %bitcast.16), calls=%async_computation.1 | async-start | bytes 6291456 | tf_op jit(solution)/shard_map/all_to_all | solution.py:421
  60.5 6.0 %copy-start = (f32[128,16,384]{2,1,0:T(8,128)}, f32[128,16,384]{2,1,0:T(8,128)S(1)}, u32[]{:S(2)}) copy-start(f32[128,16,384]{2,1,0:T(8,128)S(1)} %all-to-all-done.1) | copy-start | bytes 9437188
  60.5 36.2 %all-to-all-start = ((f32[128,16,256]{2,1,0:T(8,128)}), f32[128,16,256]{2,1,0:T(8,128)}, u32[]{:S(2)}, u32[]{:S(2)}) async-start(f32[128,16,256]{2,1,0:T(8,128)} %bitcast.17), calls=%async_computation | async-start | bytes 4194304 | tf_op jit(solution)/shard_map/all_to_all | solution.py:421
  70.3 2.7 %copy-start.4 = (bf16[16,256,768]{2,1,0:T(8,128)(2,1)}, bf16[16,256,768]{2,1,0:T(8,128)(2,1)S(1)}, u32[]{:S(2)}) copy-start(bf16[16,256,768]{2,1,0:T(8,128)(2,1)S(1)} %weights.1.refs_2_) | copy-start | bytes 18874372
  96.7 24.2 %all-to-all-start.3 = ((f32[128,16,128]{2,1,0:T(8,128)}), f32[128,16,128]{2,1,0:T(8,128)S(1)}, u32[]{:S(2)}, u32[]{:S(2)}) async-start(f32[128,16,128]{2,1,0:T(8,128)} %bitcast.18), calls=%async_computation.3 | async-start | bytes 2097152 | tf_op jit(solution)/shard_map/all_to_all | solution.py:421
  114.2 11.2 %copy-start.3 = (bf16[96,192]{1,0:T(8,128)(2,1)S(1)}, bf16[96,192]{1,0:T(8,128)(2,1)}, u32[]{:S(2)}) copy-start(bf16[96,192]{1,0:T(8,128)(2,1)} %constant.47.clone.second_ref) | copy-start | bytes 110596
  120.8 24.0 %all-to-all-start.2 = ((f32[128,16,128]{2,1,0:T(8,128)}), f32[128,16,128]{2,1,0:T(8,128)S(1)}, u32[]{:S(2)}, u32[]{:S(2)}) async-start(f32[128,16,128]{2,1,0:T(8,128)} %bitcast.19), calls=%async_computation.2 | async-start | bytes 2097152 | tf_op jit(solution)/shard_map/all_to_all | solution.py:421
  125.4 1.4 copy-start.1
  144.9 1.4 copy-start.2

commit v4 on v3

--- a/solution.py
+++ b/solution.py
@@ -27,6 +27,7 @@
 PITCH = 40
 PITCH_BACK = 72
 UNROLL = 16
+BACK_LIMIT = 51
 
 ROUND = 1.5 * 2.0**23
 ROUND_8 = ROUND * 2.0**8
@@ -192,9 +193,34 @@
     )(first, second, *[array.reshape(32, 32, -1) for array, _ in columns])
 
 
-def backward_kernel(chunk, first_ref, second_ref, x_ref, *refs):
-    before_ref = refs[0] if chunk else None
-    out_ref, middle_ref = refs[-2:]
+def backward_kernel(chunk, first_hbm, second_hbm, x_hbm, *refs):
+    before_hbm, out_hbm = (refs[0], refs[1]) if chunk else (None, None)
+    if chunk:
+        first_ref, second_ref, x_ref, middle_ref, sems, before_ref, out_ref = refs[2:]
+        out_copies = [
+            [
+                pltpu.make_async_copy(
+                    out_ref.at[e, :, pl.ds(part * 16, 16), :],
+                    out_hbm.at[e, :, pl.ds(part * 16, 16), :],
+                    sems.at[10 + 2 * part + e],
+                )
+                for e in range(2)
+            ]
+            for part in range(2)
+        ]
+        padded_ref = out_ref.reshape(2 * 32 * PITCH, 128)
+    else:
+        out_ref, first_ref, second_ref, x_ref, middle_ref, sems = refs
+    first_copies = in_parts(first_hbm, first_ref, sems, 0, 4)
+    x_copies = in_parts(x_hbm, x_ref, sems, 4, 4)
+    last_copies = [pltpu.make_async_copy(second_hbm, second_ref, sems.at[8])]
+    if chunk:
+        last_copies.append(pltpu.make_async_copy(before_hbm, before_ref, sems.at[9]))
+    for pair in zip(x_copies, first_copies):
+        for copy in pair:
+            copy.start()
+    for copy in last_copies:
+        copy.start()
     low_half = lax.broadcasted_iota(jnp.int32, (32, 128), 1) < 64
 
     def first_step(k1, carry):
@@ -203,7 +229,12 @@
         middle_ref[pl.ds(k1, 32, stride=PITCH_BACK), :] = value
         return carry
 
-    lax.fori_loop(0, 64, first_step, 0, unroll=UNROLL)
+    for part in range(4):
+        x_copies[part].wait()
+        first_copies[part].wait()
+        lax.fori_loop(part * 16, part * 16 + 16, first_step, 0, unroll=UNROLL)
+    for copy in last_copies:
+        copy.wait()
     second = second_ref[...]
 
     def second_step(m0, carry):
@@ -212,28 +243,54 @@
         value = jnp.where(value < 0.0, value + float(modulus), value) / float(modulus)
         other = pltpu.roll(value, 64, 1)
         for e in range(2):
-            place = pl.ds(e * BLOCK + m0, 32, stride=32)
+            place = pl.ds(pl.multiple_of(e * BLOCK + m0 * 32, 32), 32)
             mine = value if e == chunk else other
             if chunk:
                 mine = jnp.where(low_half, before_ref[place, :], mine)
-            out_ref[place, :] = mine
+                padded_ref[pl.ds(e * 32 * PITCH + m0, 32, stride=PITCH), :] = mine
+            else:
+                out_ref[place, :] = mine
         return carry
 
-    lax.fori_loop(0, 32, second_step, 0, unroll=UNROLL)
+    for part in range(2):
+        lax.fori_loop(part * 16, part * 16 + 16, second_step, 0, unroll=UNROLL)
+        if chunk:
+            for copy in out_copies[part]:
+                copy.start()
+    if chunk:
+        for copy in out_copies[0] + out_copies[1]:
+            copy.wait()
 
 
 def backward(values, chunk, before):
     first, second = (jnp.asarray(table, dtype=jnp.bfloat16) for table in backward_tables())
-    return pl.pallas_call(
+    last = {"out_specs": ANYWHERE} if chunk else {}
+    result = pl.pallas_call(
         functools.partial(backward_kernel, chunk),
-        out_shape=jax.ShapeDtypeStruct((2 * BLOCK, 128), jnp.float32),
-        scratch_shapes=[pltpu.VMEM((32 * PITCH_BACK, 128), jnp.float32)],
-        compiler_params=pltpu.CompilerParams(vmem_limit_bytes=32 * 2**20),
+        in_specs=[ANYWHERE] * (3 + chunk),
+        out_shape=jax.ShapeDtypeStruct(
+            (2, 32, 32, 128) if chunk else (2 * BLOCK, 128), jnp.float32
+        ),
+        scratch_shapes=[
+            pltpu.VMEM(first.shape, jnp.bfloat16),
+            pltpu.VMEM(second.shape, jnp.bfloat16),
+            pltpu.VMEM((POINTS, 128), jnp.float32),
+            pltpu.VMEM((32 * PITCH_BACK, 128), jnp.float32),
+            pltpu.SemaphoreType.DMA((14,)),
+        ]
+        + [
+            pltpu.VMEM((POINTS, 128), jnp.float32),
+            pltpu.VMEM((2, 32, PITCH, 128), jnp.float32),
+        ]
+        * chunk,
+        compiler_params=pltpu.CompilerParams(vmem_limit_bytes=BACK_LIMIT * 2**20),
         cost_estimate=pl.CostEstimate(
             flops=5 * 10**9, bytes_accessed=3 * 2**20, transcendentals=0
         ),
         name="backward",
+        **last,
     )(first, second, values, *before)
+    return result.reshape(2 * BLOCK, 128)
 
 
 def exchange_bit(tiles, index_bit, group_bit):

time: 151 us -> 149 us (0.987)
  local copies, waits for them, and re-layouts: 5.46 us -> 2.66 us
    unnamed x10 -> x6, local copies, waits for them, and re-layouts: 5.46 us -> 2.66 us
  transfers between devices with their start and end apart: 4 -> 4, of which waited for: 4 -> 4; matrix products, arithmetic and copies ran while one was open for 0% -> 0% of each run, Pallas kernels for 25% -> 26%
where the time goes in v4:
time: 149 us
  waiting for transfers between devices  69.7 us (47%)
  Pallas kernels  49.8 us (33%)
  starting transfers between devices  26.6 us (18%)
  local copies, waits for them, and re-layouts  2.66 us (2%)
    all_to_all x4, waiting for transfers between devices, exchange(): moved = lax.all_to_all(parts, AXES, split_axis=0, concat_axis=0, tiled=True)  69.7 us
    all_to_all x4, starting transfers between devices, exchange(): moved = lax.all_to_all(parts, AXES, split_axis=0, concat_axis=0, tiled=True)  26.6 us
    pallas_call x2, Pallas kernels, product(): pl.pallas_call(product_kernel, grid=(PER // STEP,), in_specs=[pl.BlockSpe...  25.6 us
    pallas_call x2, Pallas kernels, forward(): pl.pallas_call(functools.partial(forward_kernel, [tile for _, tile in col...  13.3 us
    pallas_call x2, Pallas kernels, backward(): pl.pallas_call(functools.partial(backward_kernel, chunk), in_specs=[ANYWH...  7.01 us
    pallas_call x1, Pallas kernels, weights(): pl.pallas_call(weights_kernel, grid=(PER // STEP,), in_specs=[pl.BlockSpe...  3.81 us
  transfers between devices with their start and end apart: 4, of which 4 were waited for; matrix products, arithmetic and copies ran while one was open for 0% of the time, Pallas kernels for 26%

profile of v4, /device:TPU:1, one launch (start us, length us, event | category | flops | bytes accessed | tf_op | source)
XLA Modules:
  0.0 149.0 jit_solution(11835341480977407055)
XLA Ops:
  0.0 7.5 %forward.3 = f32[2048,384]{1,0:T(8,128)} custom-call(bf16[32,192,96]{2,1,0:T(8,128)(2,1)} %constant.44.clone.first_hbm, bf16[96,96]{1,0:T(8,128)(2,1)} %constant.45.clone.second_hbm, f32[32,32,512]{2,1,0:T(8,128)} %bitcast.21, f32[32,32,512]{2,1,0:T(8,128)} %bitcast.22, f32[32,32,128]{2,1,0:T(8,128)} %bitcast.25), custom_call_target="tpu_custom_call" | custom-call | flops 8999999488 | bytes 4718592 | tf_op jit(solution)/shard_map/forward/pallas_call | solution.py:175
  7.5 11.5 %all-to-all-start.1 = ((f32[128,16,384]{2,1,0:T(8,128)}), f32[128,16,384]{2,1,0:T(8,128)S(1)}, u32[]{:S(2)}, u32[]{:S(2)}) async-start(f32[128,16,384]{2,1,0:T(8,128)} %bitcast.17), calls=%async_computation.1 | async-start | bytes 6291456 | tf_op jit(solution)/shard_map/all_to_all | solution.py:478
  19.0 5.8 %forward.2 = f32[2048,256]{1,0:T(8,128)} custom-call(bf16[32,192,96]{2,1,0:T(8,128)(2,1)} %constant.44.clone.first_hbm, bf16[96,96]{1,0:T(8,128)(2,1)} %constant.45.clone.second_hbm, f32[32,32,512]{2,1,0:T(8,128)} %bitcast.23, f32[32,32,512]{2,1,0:T(8,128)} %bitcast.24), custom_call_target="tpu_custom_call" | custom-call | flops 6000000000 | bytes 3145728 | tf_op jit(solution)/shard_map/forward/pallas_call | solution.py:175
  24.8 35.7 %all-to-all-done.1 = f32[128,16,384]{2,1,0:T(8,128)S(1)} async-done(((f32[128,16,384]{2,1,0:T(8,128)}), f32[128,16,384]{2,1,0:T(8,128)S(1)}, u32[]{:S(2)}, u32[]{:S(2)}) %all-to-all-start.1) | async-done | bytes 3145760 | tf_op jit(solution)/shard_map/all_to_all | solution.py:478
  60.5 0.0 copy-start
  60.5 5.9 %all-to-all-start = ((f32[128,16,256]{2,1,0:T(8,128)}), f32[128,16,256]{2,1,0:T(8,128)}, u32[]{:S(2)}, u32[]{:S(2)}) async-start(f32[128,16,256]{2,1,0:T(8,128)} %bitcast.18), calls=%async_computation | async-start | bytes 4194304 | tf_op jit(solution)/shard_map/all_to_all | solution.py:478
  66.5 0.0 copy-done
  66.5 3.8 %weights.1.refs_2_ = bf16[16,256,768]{2,1,0:T(8,128)(2,1)S(1)} custom-call(f32[2048,384]{1,0:T(8,128)S(1)} %bitcast.12), custom_call_target="tpu_custom_call" | custom-call | flops 3000000000 | bytes 7340032 | tf_op jit(solution)/shard_map/weights/pallas_call | solution.py:336
  70.3 0.0 copy-start.2
  70.3 2.7 %copy-done.2 = bf16[16,256,768]{2,1,0:T(8,128)(2,1)} copy-done((bf16[16,256,768]{2,1,0:T(8,128)(2,1)}, bf16[16,256,768]{2,1,0:T(8,128)(2,1)S(1)}, u32[]{:S(2)}) %copy-start.2) | copy-done | bytes 6291480
  73.0 12.8 %product.3 = f32[2048,128]{1,0:T(8,128)} custom-call(f32[1]{0:T(128)} %bitcast.sign_ref, f32[2048,384]{1,0:T(8,128)} %bitcast.13, f32[2048,384]{1,0:T(8,128)} %bitcast.14, bf16[16,256,768]{2,1,0:T(8,128)(2,1)} %copy-done.2), custom_call_target="tpu_custom_call" | custom-call | flops 12000000000 | bytes 9437184 | tf_op jit(solution)/shard_map/product/pallas_call | solution.py:458
  85.8 10.9 %all-to-all-done = f32[128,16,256]{2,1,0:T(8,128)} async-done(((f32[128,16,256]{2,1,0:T(8,128)}), f32[128,16,256]{2,1,0:T(8,128)}, u32[]{:S(2)}, u32[]{:S(2)}) %all-to-all-start) | async-done | bytes 2097184 | tf_op jit(solution)/shard_map/all_to_all | solution.py:478
  96.7 4.7 %all-to-all-start.3 = ((f32[128,16,128]{2,1,0:T(8,128)}), f32[128,16,128]{2,1,0:T(8,128)S(1)}, u32[]{:S(2)}, u32[]{:S(2)}) async-start(f32[128,16,128]{2,1,0:T(8,128)} %bitcast.19), calls=%async_computation.3 | async-start | bytes 2097152 | tf_op jit(solution)/shard_map/all_to_all | solution.py:478
  101.3 12.8 %product.2 = f32[2048,128]{1,0:T(8,128)} custom-call(f32[1]{0:T(128)} %bitcast.sign_ref, f32[2048,256]{1,0:T(8,128)} %bitcast.3.refs_0_.refs_1_, f32[2048,256]{1,0:T(8,128)} %bitcast.3.refs_0_.refs_1_, bf16[16,256,768]{2,1,0:T(8,128)(2,1)} %copy-done.2), custom_call_target="tpu_custom_call" | custom-call | flops 12000000000 | bytes 9437184 | tf_op jit(solution)/shard_map/product/pallas_call | solution.py:458
  114.2 0.0 copy-start.1
  114.2 6.7 %all-to-all-done.3 = f32[128,16,128]{2,1,0:T(8,128)S(1)} async-done(((f32[128,16,128]{2,1,0:T(8,128)}), f32[128,16,128]{2,1,0:T(8,128)S(1)}, u32[]{:S(2)}, u32[]{:S(2)}) %all-to-all-start.3) | async-done | bytes 1048608 | tf_op jit(solution)/shard_map/all_to_all | solution.py:478
  120.8 4.5 %all-to-all-start.2 = ((f32[128,16,128]{2,1,0:T(8,128)}), f32[128,16,128]{2,1,0:T(8,128)S(1)}, u32[]{:S(2)}, u32[]{:S(2)}) async-start(f32[128,16,128]{2,1,0:T(8,128)} %bitcast.20), calls=%async_computation.2 | async-start | bytes 2097152 | tf_op jit(solution)/shard_map/all_to_all | solution.py:478
  125.4 0.0 copy-done.1
  125.4 3.1 %backward.2.refs_0_ = f32[2048,128]{1,0:T(8,128)S(1)} custom-call(bf16[64,96,96]{2,1,0:T(8,128)(2,1)} %constant.46.clone.first_hbm, bf16[96,192]{1,0:T(8,128)(2,1)S(1)} %copy-done.1, f32[2048,128]{1,0:T(8,128)S(1)} %bitcast.15), custom_call_target="tpu_custom_call" | custom-call | flops 5000000000 | bytes 3145728 | tf_op jit(solution)/shard_map/backward/pallas_call | solution.py:268
  128.4 16.4 %all-to-all-done.2 = f32[128,16,128]{2,1,0:T(8,128)S(1)} async-done(((f32[128,16,128]{2,1,0:T(8,128)}), f32[128,16,128]{2,1,0:T(8,128)S(1)}, u32[]{:S(2)}, u32[]{:S(2)}) %all-to-all-start.2) | async-done | bytes 1048608 | tf_op jit(solution)/shard_map/all_to_all | solution.py:478
  144.9 3.9 %backward.3 = f32[2,32,32,128]{3,2,1,0:T(8,128)} custom-call(bf16[64,96,96]{2,1,0:T(8,128)(2,1)} %constant.46.clone.first_hbm, bf16[96,192]{1,0:T(8,128)(2,1)S(1)} %copy-done.1, f32[2048,128]{1,0:T(8,128)S(1)} %bitcast.16, f32[2048,128]{1,0:T(8,128)S(1)} %backward.2.refs_0_), custom_call_target="tpu_custom_call" | custom-call | flops 5000000000 | bytes 3145728 | tf_op jit(solution)/shard_map/backward/pallas_call | solution.py:268
Async XLA Ops:
  7.5 53.0 %all-to-all-start.1 = ((f32[128,16,384]{2,1,0:T(8,128)}), f32[128,16,384]{2,1,0:T(8,128)S(1)}, u32[]{:S(2)}, u32[]{:S(2)}) async-start(f32[128,16,384]{2,1,0:T(8,128)} %bitcast.17), calls=%async_computation.1 | async-start | bytes 6291456 | tf_op jit(solution)/shard_map/all_to_all | solution.py:478
  60.5 6.0 %copy-start = (f32[128,16,384]{2,1,0:T(8,128)}, f32[128,16,384]{2,1,0:T(8,128)S(1)}, u32[]{:S(2)}) copy-start(f32[128,16,384]{2,1,0:T(8,128)S(1)} %all-to-all-done.1) | copy-start | bytes 9437188
  60.5 36.2 %all-to-all-start = ((f32[128,16,256]{2,1,0:T(8,128)}), f32[128,16,256]{2,1,0:T(8,128)}, u32[]{:S(2)}, u32[]{:S(2)}) async-start(f32[128,16,256]{2,1,0:T(8,128)} %bitcast.18), calls=%async_computation | async-start | bytes 4194304 | tf_op jit(solution)/shard_map/all_to_all | solution.py:478
  70.3 2.7 %copy-start.2 = (bf16[16,256,768]{2,1,0:T(8,128)(2,1)}, bf16[16,256,768]{2,1,0:T(8,128)(2,1)S(1)}, u32[]{:S(2)}) copy-start(bf16[16,256,768]{2,1,0:T(8,128)(2,1)S(1)} %weights.1.refs_2_) | copy-start | bytes 18874372
  96.7 24.2 %all-to-all-start.3 = ((f32[128,16,128]{2,1,0:T(8,128)}), f32[128,16,128]{2,1,0:T(8,128)S(1)}, u32[]{:S(2)}, u32[]{:S(2)}) async-start(f32[128,16,128]{2,1,0:T(8,128)} %bitcast.19), calls=%async_computation.3 | async-start | bytes 2097152 | tf_op jit(solution)/shard_map/all_to_all | solution.py:478
  114.2 11.2 %copy-start.1 = (bf16[96,192]{1,0:T(8,128)(2,1)S(1)}, bf16[96,192]{1,0:T(8,128)(2,1)}, u32[]{:S(2)}) copy-start(bf16[96,192]{1,0:T(8,128)(2,1)} %constant.47.clone.second_hbm) | copy-start | bytes 110596
  120.8 24.0 %all-to-all-start.2 = ((f32[128,16,128]{2,1,0:T(8,128)}), f32[128,16,128]{2,1,0:T(8,128)S(1)}, u32[]{:S(2)}, u32[]{:S(2)}) async-start(f32[128,16,128]{2,1,0:T(8,128)} %bitcast.20), calls=%async_computation.2 | async-start | bytes 2097152 | tf_op jit(solution)/shard_map/all_to_all | solution.py:478

commit v5 on v4

--- a/solution.py
+++ b/solution.py
@@ -52,7 +52,7 @@
         value = (value - low) >> 8
         middle = ((value + 128) & 255) - 128
         high = (value - middle) >> 8
-        rows = np.concatenate([low, middle, high], axis=-2)
+        rows = np.concatenate([low, middle * 2.0**8, high * 2.0**16], axis=-2)
         columns.append(rows * 2.0 ** (-8 * a))
     return np.concatenate(columns, axis=-1).astype(np.float32)
 
@@ -88,9 +88,8 @@
 
 def fold(sums):
     s0, s1, s2 = sums
-    quotient = s2 * (65536.0 / modulus) + s1 * (256.0 / modulus)
-    quotient = (quotient + ROUND) - ROUND
-    return ((s2 * 65536.0 - quotient * HIGH) + s1 * 256.0) + (s0 - quotient)
+    quotient = ((s2 + s1) * (1.0 / modulus) + ROUND) - ROUND
+    return ((s2 - quotient * HIGH) + s1) + (s0 - quotient)
 
 
 def times_256(value):

time: 149 us -> 149 us (level)
  Pallas kernels: 49.8 us -> 48.3 us
  transfers between devices with their start and end apart: 4 -> 4, of which waited for: 4 -> 4; matrix products, arithmetic and copies ran while one was open for 0% -> 0% of each run, Pallas kernels for 26% -> 25%
where the time goes in v5:
time: 149 us; the launch traced here: 148 us
  waiting for transfers between devices  70.4 us (47%)
  Pallas kernels  48.3 us (32%)
  starting transfers between devices  26.8 us (18%)
  local copies, waits for them, and re-layouts  2.66 us (2%)
    all_to_all x4, waiting for transfers between devices, exchange(): moved = lax.all_to_all(parts, AXES, split_axis=0, concat_axis=0, tiled=True)  70.4 us
    all_to_all x4, starting transfers between devices, exchange(): moved = lax.all_to_all(parts, AXES, split_axis=0, concat_axis=0, tiled=True)  26.8 us
    pallas_call x2, Pallas kernels, product(): pl.pallas_call(product_kernel, grid=(PER // STEP,), in_specs=[pl.BlockSpe...  25.7 us
    pallas_call x2, Pallas kernels, forward(): pl.pallas_call(functools.partial(forward_kernel, [tile for _, tile in col...  12 us
    pallas_call x2, Pallas kernels, backward(): pl.pallas_call(functools.partial(backward_kernel, chunk), in_specs=[ANYWH...  6.87 us
    pallas_call x1, Pallas kernels, weights(): pl.pallas_call(weights_kernel, grid=(PER // STEP,), in_specs=[pl.BlockSpe...  3.81 us
  transfers between devices with their start and end apart: 4, of which 4 were waited for; matrix products, arithmetic and copies ran while one was open for 0% of the time, Pallas kernels for 25%

profile of v5, /device:TPU:1, one launch (start us, length us, event | category | flops | bytes accessed | tf_op | source)
XLA Modules:
  0.0 148.4 jit_solution(1254067580910076498)
XLA Ops:
  0.0 6.8 %forward.3 = f32[2048,384]{1,0:T(8,128)} custom-call(bf16[32,192,96]{2,1,0:T(8,128)(2,1)} %constant.44.clone.first_hbm, bf16[96,96]{1,0:T(8,128)(2,1)} %constant.45.clone.second_hbm, f32[32,32,512]{2,1,0:T(8,128)} %bitcast.21, f32[32,32,512]{2,1,0:T(8,128)} %bitcast.22, f32[32,32,128]{2,1,0:T(8,128)} %bitcast.25), custom_call_target="tpu_custom_call" | custom-call | flops 8999999488 | bytes 4718592 | tf_op jit(solution)/shard_map/forward/pallas_call | solution.py:174
  6.8 11.5 %all-to-all-start.1 = ((f32[128,16,384]{2,1,0:T(8,128)}), f32[128,16,384]{2,1,0:T(8,128)S(1)}, u32[]{:S(2)}, u32[]{:S(2)}) async-start(f32[128,16,384]{2,1,0:T(8,128)} %bitcast.17), calls=%async_computation.1 | async-start | bytes 6291456 | tf_op jit(solution)/shard_map/all_to_all | solution.py:477
  18.3 5.2 %forward.2 = f32[2048,256]{1,0:T(8,128)} custom-call(bf16[32,192,96]{2,1,0:T(8,128)(2,1)} %constant.44.clone.first_hbm, bf16[96,96]{1,0:T(8,128)(2,1)} %constant.45.clone.second_hbm, f32[32,32,512]{2,1,0:T(8,128)} %bitcast.23, f32[32,32,512]{2,1,0:T(8,128)} %bitcast.24), custom_call_target="tpu_custom_call" | custom-call | flops 6000000000 | bytes 3145728 | tf_op jit(solution)/shard_map/forward/pallas_call | solution.py:174
  23.5 36.3 %all-to-all-done.1 = f32[128,16,384]{2,1,0:T(8,128)S(1)} async-done(((f32[128,16,384]{2,1,0:T(8,128)}), f32[128,16,384]{2,1,0:T(8,128)S(1)}, u32[]{:S(2)}, u32[]{:S(2)}) %all-to-all-start.1) | async-done | bytes 3145760 | tf_op jit(solution)/shard_map/all_to_all | solution.py:477
  59.8 0.0 copy-start
  59.8 5.9 %all-to-all-start = ((f32[128,16,256]{2,1,0:T(8,128)}), f32[128,16,256]{2,1,0:T(8,128)}, u32[]{:S(2)}, u32[]{:S(2)}) async-start(f32[128,16,256]{2,1,0:T(8,128)} %bitcast.18), calls=%async_computation | async-start | bytes 4194304 | tf_op jit(solution)/shard_map/all_to_all | solution.py:477
  65.8 0.0 copy-done
  65.8 3.8 %weights.1.refs_2_ = bf16[16,256,768]{2,1,0:T(8,128)(2,1)S(1)} custom-call(f32[2048,384]{1,0:T(8,128)S(1)} %bitcast.12), custom_call_target="tpu_custom_call" | custom-call | flops 3000000000 | bytes 7340032 | tf_op jit(solution)/shard_map/weights/pallas_call | solution.py:335
  69.7 0.0 copy-start.2
  69.7 2.7 %copy-done.2 = bf16[16,256,768]{2,1,0:T(8,128)(2,1)} copy-done((bf16[16,256,768]{2,1,0:T(8,128)(2,1)}, bf16[16,256,768]{2,1,0:T(8,128)(2,1)S(1)}, u32[]{:S(2)}) %copy-start.2) | copy-done | bytes 6291480
  72.3 12.9 %product.3 = f32[2048,128]{1,0:T(8,128)} custom-call(f32[1]{0:T(128)} %bitcast.sign_ref, f32[2048,384]{1,0:T(8,128)} %bitcast.13, f32[2048,384]{1,0:T(8,128)} %bitcast.14, bf16[16,256,768]{2,1,0:T(8,128)(2,1)} %copy-done.2), custom_call_target="tpu_custom_call" | custom-call | flops 12000000000 | bytes 9437184 | tf_op jit(solution)/shard_map/product/pallas_call | solution.py:457
  85.2 10.9 %all-to-all-done = f32[128,16,256]{2,1,0:T(8,128)} async-done(((f32[128,16,256]{2,1,0:T(8,128)}), f32[128,16,256]{2,1,0:T(8,128)}, u32[]{:S(2)}, u32[]{:S(2)}) %all-to-all-start) | async-done | bytes 2097184 | tf_op jit(solution)/shard_map/all_to_all | solution.py:477
  96.0 4.6 %all-to-all-start.3 = ((f32[128,16,128]{2,1,0:T(8,128)}), f32[128,16,128]{2,1,0:T(8,128)S(1)}, u32[]{:S(2)}, u32[]{:S(2)}) async-start(f32[128,16,128]{2,1,0:T(8,128)} %bitcast.19), calls=%async_computation.3 | async-start | bytes 2097152 | tf_op jit(solution)/shard_map/all_to_all | solution.py:477
  100.7 12.8 %product.2 = f32[2048,128]{1,0:T(8,128)} custom-call(f32[1]{0:T(128)} %bitcast.sign_ref, f32[2048,256]{1,0:T(8,128)} %bitcast.3.refs_0_.refs_1_, f32[2048,256]{1,0:T(8,128)} %bitcast.3.refs_0_.refs_1_, bf16[16,256,768]{2,1,0:T(8,128)(2,1)} %copy-done.2), custom_call_target="tpu_custom_call" | custom-call | flops 12000000000 | bytes 9437184 | tf_op jit(solution)/shard_map/product/pallas_call | solution.py:457
  113.5 0.0 copy-start.1
  113.5 6.7 %all-to-all-done.3 = f32[128,16,128]{2,1,0:T(8,128)S(1)} async-done(((f32[128,16,128]{2,1,0:T(8,128)}), f32[128,16,128]{2,1,0:T(8,128)S(1)}, u32[]{:S(2)}, u32[]{:S(2)}) %all-to-all-start.3) | async-done | bytes 1048608 | tf_op jit(solution)/shard_map/all_to_all | solution.py:477
  120.2 4.7 %all-to-all-start.2 = ((f32[128,16,128]{2,1,0:T(8,128)}), f32[128,16,128]{2,1,0:T(8,128)S(1)}, u32[]{:S(2)}, u32[]{:S(2)}) async-start(f32[128,16,128]{2,1,0:T(8,128)} %bitcast.20), calls=%async_computation.2 | async-start | bytes 2097152 | tf_op jit(solution)/shard_map/all_to_all | solution.py:477
  124.9 0.0 copy-done.1
  124.9 3.0 %backward.2.refs_0_ = f32[2048,128]{1,0:T(8,128)S(1)} custom-call(bf16[64,96,96]{2,1,0:T(8,128)(2,1)} %constant.46.clone.first_hbm, bf16[96,192]{1,0:T(8,128)(2,1)S(1)} %copy-done.1, f32[2048,128]{1,0:T(8,128)S(1)} %bitcast.15), custom_call_target="tpu_custom_call" | custom-call | flops 5000000000 | bytes 3145728 | tf_op jit(solution)/shard_map/backward/pallas_call | solution.py:267
  127.9 16.5 %all-to-all-done.2 = f32[128,16,128]{2,1,0:T(8,128)S(1)} async-done(((f32[128,16,128]{2,1,0:T(8,128)}), f32[128,16,128]{2,1,0:T(8,128)S(1)}, u32[]{:S(2)}, u32[]{:S(2)}) %all-to-all-start.2) | async-done | bytes 1048608 | tf_op jit(solution)/shard_map/all_to_all | solution.py:477
  144.4 3.9 %backward.3 = f32[2,32,32,128]{3,2,1,0:T(8,128)} custom-call(bf16[64,96,96]{2,1,0:T(8,128)(2,1)} %constant.46.clone.first_hbm, bf16[96,192]{1,0:T(8,128)(2,1)S(1)} %copy-done.1, f32[2048,128]{1,0:T(8,128)S(1)} %bitcast.16, f32[2048,128]{1,0:T(8,128)S(1)} %backward.2.refs_0_), custom_call_target="tpu_custom_call" | custom-call | flops 5000000000 | bytes 3145728 | tf_op jit(solution)/shard_map/backward/pallas_call | solution.py:267
Async XLA Ops:
  6.8 53.0 %all-to-all-start.1 = ((f32[128,16,384]{2,1,0:T(8,128)}), f32[128,16,384]{2,1,0:T(8,128)S(1)}, u32[]{:S(2)}, u32[]{:S(2)}) async-start(f32[128,16,384]{2,1,0:T(8,128)} %bitcast.17), calls=%async_computation.1 | async-start | bytes 6291456 | tf_op jit(solution)/shard_map/all_to_all | solution.py:477
  59.8 6.0 %copy-start = (f32[128,16,384]{2,1,0:T(8,128)}, f32[128,16,384]{2,1,0:T(8,128)S(1)}, u32[]{:S(2)}) copy-start(f32[128,16,384]{2,1,0:T(8,128)S(1)} %all-to-all-done.1) | copy-start | bytes 9437188
  59.8 36.2 %all-to-all-start = ((f32[128,16,256]{2,1,0:T(8,128)}), f32[128,16,256]{2,1,0:T(8,128)}, u32[]{:S(2)}, u32[]{:S(2)}) async-start(f32[128,16,256]{2,1,0:T(8,128)} %bitcast.18), calls=%async_computation | async-start | bytes 4194304 | tf_op jit(solution)/shard_map/all_to_all | solution.py:477
  69.7 2.7 %copy-start.2 = (bf16[16,256,768]{2,1,0:T(8,128)(2,1)}, bf16[16,256,768]{2,1,0:T(8,128)(2,1)S(1)}, u32[]{:S(2)}) copy-start(bf16[16,256,768]{2,1,0:T(8,128)(2,1)S(1)} %weights.1.refs_2_) | copy-start | bytes 18874372
  96.0 24.2 %all-to-all-start.3 = ((f32[128,16,128]{2,1,0:T(8,128)}), f32[128,16,128]{2,1,0:T(8,128)S(1)}, u32[]{:S(2)}, u32[]{:S(2)}) async-start(f32[128,16,128]{2,1,0:T(8,128)} %bitcast.19), calls=%async_computation.3 | async-start | bytes 2097152 | tf_op jit(solution)/shard_map/all_to_all | solution.py:477
  113.5 11.4 %copy-start.1 = (bf16[96,192]{1,0:T(8,128)(2,1)S(1)}, bf16[96,192]{1,0:T(8,128)(2,1)}, u32[]{:S(2)}) copy-start(bf16[96,192]{1,0:T(8,128)(2,1)} %constant.47.clone.second_hbm) | copy-start | bytes 110596
  120.2 24.2 %all-to-all-start.2 = ((f32[128,16,128]{2,1,0:T(8,128)}), f32[128,16,128]{2,1,0:T(8,128)S(1)}, u32[]{:S(2)}, u32[]{:S(2)}) async-start(f32[128,16,128]{2,1,0:T(8,128)} %bitcast.20), calls=%async_computation.2 | async-start | bytes 2097152 | tf_op jit(solution)/shard_map/all_to_all | solution.py:477

commit v6 on v5

--- a/solution.py
+++ b/solution.py
@@ -129,10 +129,10 @@
         )
         for index, (x_hbm, x_ref, tile) in enumerate(zip(x_hbms, x_refs, columns))
     ]
-    first_copies = in_parts(first_hbm, first_ref, sems, tiles, 2)
-    second_copy = pltpu.make_async_copy(second_hbm, second_ref, sems.at[tiles + 2])
-    out_copies = in_parts(out_ref, out_hbm, sems, tiles + 3, 4)
-    for copy in x_copies + first_copies + [second_copy]:
+    first_copies = in_parts(first_hbm, first_ref, sems, tiles, 4)
+    second_copy = pltpu.make_async_copy(second_hbm, second_ref, sems.at[tiles + 4])
+    out_copies = in_parts(out_ref, out_hbm, sems, tiles + 5, 8)
+    for copy in first_copies[:1] + x_copies + first_copies[1:] + [second_copy]:
         copy.start()
     for copy in x_copies:
         copy.wait()
@@ -145,9 +145,9 @@
             ref[pl.ds(m0, 64, stride=PITCH), :] = value[:, 128 * tile : 128 * tile + 128]
         return carry
 
-    for part in range(2):
+    for part in range(4):
         first_copies[part].wait()
-        lax.fori_loop(part * 16, part * 16 + 16, first_step, 0, unroll=UNROLL)
+        lax.fori_loop(part * 8, part * 8 + 8, first_step, 0, unroll=8)
     second_copy.wait()
     second = second_ref[...]
 
@@ -158,8 +158,8 @@
         out_ref[rows, :] = fold(thirds(matmul(second, digit_rows(value))))
         return carry
 
-    for part in range(4):
-        lax.fori_loop(part * 16, part * 16 + 16, second_step, 0, unroll=UNROLL)
+    for part in range(8):
+        lax.fori_loop(part * 8, part * 8 + 8, second_step, 0, unroll=8)
         out_copies[part].start()
     for copy in out_copies:
         copy.wait()
@@ -183,7 +183,7 @@
         ]
         + [pltpu.VMEM((32, PITCH, 128), jnp.float32)] * tiles
         + [pltpu.VMEM((64 * PITCH, 128), jnp.float32)] * tiles
-        + [pltpu.SemaphoreType.DMA((tiles + 7,))],
+        + [pltpu.SemaphoreType.DMA((tiles + 13,))],
         compiler_params=pltpu.CompilerParams(vmem_limit_bytes=60 * 2**20),
         cost_estimate=pl.CostEstimate(
             flops=tiles * 3 * 10**9, bytes_accessed=tiles * 3 * 2**19, transcendentals=0
@@ -239,7 +239,7 @@
     def second_step(m0, carry):
         rows = pl.ds(pl.multiple_of(m0 * PITCH_BACK, 8), 64)
         value = fold(thirds(matmul(second, digit_rows(middle_ref[rows, :]))))
-        value = jnp.where(value < 0.0, value + float(modulus), value) / float(modulus)
+        value = jnp.where(value < 0.0, value + float(modulus), value) * (1.0 / modulus)
         other = pltpu.roll(value, 64, 1)
         for e in range(2):
             place = pl.ds(pl.multiple_of(e * BLOCK + m0 * 32, 32), 32)

time: 149 us -> 149 us (level)
  no operation moved by 1% of the time
where the time goes in v6:
time: 149 us; the launch traced here: 148 us
  waiting for transfers between devices  70.3 us (47%)
  Pallas kernels  48.4 us (32%)
  starting transfers between devices  26.8 us (18%)
  local copies, waits for them, and re-layouts  2.66 us (2%)
    all_to_all x4, waiting for transfers between devices, exchange(): moved = lax.all_to_all(parts, AXES, split_axis=0, concat_axis=0, tiled=True)  70.3 us
    all_to_all x4, starting transfers between devices, exchange(): moved = lax.all_to_all(parts, AXES, split_axis=0, concat_axis=0, tiled=True)  26.8 us
    pallas_call x2, Pallas kernels, product(): pl.pallas_call(product_kernel, grid=(PER // STEP,), in_specs=[pl.BlockSpe...  25.6 us
    pallas_call x2, Pallas kernels, forward(): pl.pallas_call(functools.partial(forward_kernel, [tile for _, tile in col...  12.1 us
    pallas_call x2, Pallas kernels, backward(): pl.pallas_call(functools.partial(backward_kernel, chunk), in_specs=[ANYWH...  6.87 us
    pallas_call x1, Pallas kernels, weights(): pl.pallas_call(weights_kernel, grid=(PER // STEP,), in_specs=[pl.BlockSpe...  3.81 us
  transfers between devices with their start and end apart: 4, of which 4 were waited for; matrix products, arithmetic and copies ran while one was open for 0% of the time, Pallas kernels for 25%

profile of v6, /device:TPU:1, one launch (start us, length us, event | category | flops | bytes accessed | tf_op | source)
XLA Modules:
  0.0 148.4 jit_solution(5597621557864878965)
XLA Ops:
  0.0 6.8 %forward.3 = f32[2048,384]{1,0:T(8,128)} custom-call(bf16[32,192,96]{2,1,0:T(8,128)(2,1)} %constant.44.clone.first_hbm, bf16[96,96]{1,0:T(8,128)(2,1)} %constant.45.clone.second_hbm, f32[32,32,512]{2,1,0:T(8,128)} %bitcast.21, f32[32,32,512]{2,1,0:T(8,128)} %bitcast.22, f32[32,32,128]{2,1,0:T(8,128)} %bitcast.25), custom_call_target="tpu_custom_call" | custom-call | flops 8999999488 | bytes 4718592 | tf_op jit(solution)/shard_map/forward/pallas_call | solution.py:174
  6.8 11.5 %all-to-all-start.1 = ((f32[128,16,384]{2,1,0:T(8,128)}), f32[128,16,384]{2,1,0:T(8,128)S(1)}, u32[]{:S(2)}, u32[]{:S(2)}) async-start(f32[128,16,384]{2,1,0:T(8,128)} %bitcast.17), calls=%async_computation.1 | async-start | bytes 6291456 | tf_op jit(solution)/shard_map/all_to_all | solution.py:477
  18.3 5.3 %forward.2 = f32[2048,256]{1,0:T(8,128)} custom-call(bf16[32,192,96]{2,1,0:T(8,128)(2,1)} %constant.44.clone.first_hbm, bf16[96,96]{1,0:T(8,128)(2,1)} %constant.45.clone.second_hbm, f32[32,32,512]{2,1,0:T(8,128)} %bitcast.23, f32[32,32,512]{2,1,0:T(8,128)} %bitcast.24), custom_call_target="tpu_custom_call" | custom-call | flops 6000000000 | bytes 3145728 | tf_op jit(solution)/shard_map/forward/pallas_call | solution.py:174
  23.6 36.2 %all-to-all-done.1 = f32[128,16,384]{2,1,0:T(8,128)S(1)} async-done(((f32[128,16,384]{2,1,0:T(8,128)}), f32[128,16,384]{2,1,0:T(8,128)S(1)}, u32[]{:S(2)}, u32[]{:S(2)}) %all-to-all-start.1) | async-done | bytes 3145760 | tf_op jit(solution)/shard_map/all_to_all | solution.py:477
  59.8 0.0 copy-start
  59.8 5.9 %all-to-all-start = ((f32[128,16,256]{2,1,0:T(8,128)}), f32[128,16,256]{2,1,0:T(8,128)}, u32[]{:S(2)}, u32[]{:S(2)}) async-start(f32[128,16,256]{2,1,0:T(8,128)} %bitcast.18), calls=%async_computation | async-start | bytes 4194304 | tf_op jit(solution)/shard_map/all_to_all | solution.py:477
  65.8 0.0 copy-done
  65.8 3.8 %weights.1.refs_2_ = bf16[16,256,768]{2,1,0:T(8,128)(2,1)S(1)} custom-call(f32[2048,384]{1,0:T(8,128)S(1)} %bitcast.12), custom_call_target="tpu_custom_call" | custom-call | flops 3000000000 | bytes 7340032 | tf_op jit(solution)/shard_map/weights/pallas_call | solution.py:335
  69.6 0.0 copy-start.2
  69.7 2.7 %copy-done.2 = bf16[16,256,768]{2,1,0:T(8,128)(2,1)} copy-done((bf16[16,256,768]{2,1,0:T(8,128)(2,1)}, bf16[16,256,768]{2,1,0:T(8,128)(2,1)S(1)}, u32[]{:S(2)}) %copy-start.2) | copy-done | bytes 6291480
  72.3 12.8 %product.3 = f32[2048,128]{1,0:T(8,128)} custom-call(f32[1]{0:T(128)} %bitcast.sign_ref, f32[2048,384]{1,0:T(8,128)} %bitcast.13, f32[2048,384]{1,0:T(8,128)} %bitcast.14, bf16[16,256,768]{2,1,0:T(8,128)(2,1)} %copy-done.2), custom_call_target="tpu_custom_call" | custom-call | flops 12000000000 | bytes 9437184 | tf_op jit(solution)/shard_map/product/pallas_call | solution.py:457
  85.1 10.9 %all-to-all-done = f32[128,16,256]{2,1,0:T(8,128)} async-done(((f32[128,16,256]{2,1,0:T(8,128)}), f32[128,16,256]{2,1,0:T(8,128)}, u32[]{:S(2)}, u32[]{:S(2)}) %all-to-all-start) | async-done | bytes 2097184 | tf_op jit(solution)/shard_map/all_to_all | solution.py:477
  96.0 4.6 %all-to-all-start.3 = ((f32[128,16,128]{2,1,0:T(8,128)}), f32[128,16,128]{2,1,0:T(8,128)S(1)}, u32[]{:S(2)}, u32[]{:S(2)}) async-start(f32[128,16,128]{2,1,0:T(8,128)} %bitcast.19), calls=%async_computation.3 | async-start | bytes 2097152 | tf_op jit(solution)/shard_map/all_to_all | solution.py:477
  100.7 12.8 %product.2 = f32[2048,128]{1,0:T(8,128)} custom-call(f32[1]{0:T(128)} %bitcast.sign_ref, f32[2048,256]{1,0:T(8,128)} %bitcast.3.refs_0_.refs_1_, f32[2048,256]{1,0:T(8,128)} %bitcast.3.refs_0_.refs_1_, bf16[16,256,768]{2,1,0:T(8,128)(2,1)} %copy-done.2), custom_call_target="tpu_custom_call" | custom-call | flops 12000000000 | bytes 9437184 | tf_op jit(solution)/shard_map/product/pallas_call | solution.py:457
  113.5 0.0 copy-start.1
  113.5 6.7 %all-to-all-done.3 = f32[128,16,128]{2,1,0:T(8,128)S(1)} async-done(((f32[128,16,128]{2,1,0:T(8,128)}), f32[128,16,128]{2,1,0:T(8,128)S(1)}, u32[]{:S(2)}, u32[]{:S(2)}) %all-to-all-start.3) | async-done | bytes 1048608 | tf_op jit(solution)/shard_map/all_to_all | solution.py:477
  120.2 4.7 %all-to-all-start.2 = ((f32[128,16,128]{2,1,0:T(8,128)}), f32[128,16,128]{2,1,0:T(8,128)S(1)}, u32[]{:S(2)}, u32[]{:S(2)}) async-start(f32[128,16,128]{2,1,0:T(8,128)} %bitcast.20), calls=%async_computation.2 | async-start | bytes 2097152 | tf_op jit(solution)/shard_map/all_to_all | solution.py:477
  124.9 0.0 copy-done.1
  124.9 3.0 %backward.2.refs_0_ = f32[2048,128]{1,0:T(8,128)S(1)} custom-call(bf16[64,96,96]{2,1,0:T(8,128)(2,1)} %constant.46.clone.first_hbm, bf16[96,192]{1,0:T(8,128)(2,1)S(1)} %copy-done.1, f32[2048,128]{1,0:T(8,128)S(1)} %bitcast.15), custom_call_target="tpu_custom_call" | custom-call | flops 5000000000 | bytes 3145728 | tf_op jit(solution)/shard_map/backward/pallas_call | solution.py:267
  127.9 16.5 %all-to-all-done.2 = f32[128,16,128]{2,1,0:T(8,128)S(1)} async-done(((f32[128,16,128]{2,1,0:T(8,128)}), f32[128,16,128]{2,1,0:T(8,128)S(1)}, u32[]{:S(2)}, u32[]{:S(2)}) %all-to-all-start.2) | async-done | bytes 1048608 | tf_op jit(solution)/shard_map/all_to_all | solution.py:477
  144.4 3.9 %backward.3 = f32[2,32,32,128]{3,2,1,0:T(8,128)} custom-call(bf16[64,96,96]{2,1,0:T(8,128)(2,1)} %constant.46.clone.first_hbm, bf16[96,192]{1,0:T(8,128)(2,1)S(1)} %copy-done.1, f32[2048,128]{1,0:T(8,128)S(1)} %bitcast.16, f32[2048,128]{1,0:T(8,128)S(1)} %backward.2.refs_0_), custom_call_target="tpu_custom_call" | custom-call | flops 5000000000 | bytes 3145728 | tf_op jit(solution)/shard_map/backward/pallas_call | solution.py:267
Async XLA Ops:
  6.8 53.0 %all-to-all-start.1 = ((f32[128,16,384]{2,1,0:T(8,128)}), f32[128,16,384]{2,1,0:T(8,128)S(1)}, u32[]{:S(2)}, u32[]{:S(2)}) async-start(f32[128,16,384]{2,1,0:T(8,128)} %bitcast.17), calls=%async_computation.1 | async-start | bytes 6291456 | tf_op jit(solution)/shard_map/all_to_all | solution.py:477
  59.8 6.0 %copy-start = (f32[128,16,384]{2,1,0:T(8,128)}, f32[128,16,384]{2,1,0:T(8,128)S(1)}, u32[]{:S(2)}) copy-start(f32[128,16,384]{2,1,0:T(8,128)S(1)} %all-to-all-done.1) | copy-start | bytes 9437188
  59.8 36.2 %all-to-all-start = ((f32[128,16,256]{2,1,0:T(8,128)}), f32[128,16,256]{2,1,0:T(8,128)}, u32[]{:S(2)}, u32[]{:S(2)}) async-start(f32[128,16,256]{2,1,0:T(8,128)} %bitcast.18), calls=%async_computation | async-start | bytes 4194304 | tf_op jit(solution)/shard_map/all_to_all | solution.py:477
  69.6 2.7 %copy-start.2 = (bf16[16,256,768]{2,1,0:T(8,128)(2,1)}, bf16[16,256,768]{2,1,0:T(8,128)(2,1)S(1)}, u32[]{:S(2)}) copy-start(bf16[16,256,768]{2,1,0:T(8,128)(2,1)S(1)} %weights.1.refs_2_) | copy-start | bytes 18874372
  96.0 24.2 %all-to-all-start.3 = ((f32[128,16,128]{2,1,0:T(8,128)}), f32[128,16,128]{2,1,0:T(8,128)S(1)}, u32[]{:S(2)}, u32[]{:S(2)}) async-start(f32[128,16,128]{2,1,0:T(8,128)} %bitcast.19), calls=%async_computation.3 | async-start | bytes 2097152 | tf_op jit(solution)/shard_map/all_to_all | solution.py:477
  113.5 11.4 %copy-start.1 = (bf16[96,192]{1,0:T(8,128)(2,1)S(1)}, bf16[96,192]{1,0:T(8,128)(2,1)}, u32[]{:S(2)}) copy-start(bf16[96,192]{1,0:T(8,128)(2,1)} %constant.47.clone.second_hbm) | copy-start | bytes 110596
  120.2 24.2 %all-to-all-start.2 = ((f32[128,16,128]{2,1,0:T(8,128)}), f32[128,16,128]{2,1,0:T(8,128)S(1)}, u32[]{:S(2)}, u32[]{:S(2)}) async-start(f32[128,16,128]{2,1,0:T(8,128)} %bitcast.20), calls=%async_computation.2 | async-start | bytes 2097152 | tf_op jit(solution)/shard_map/all_to_all | solution.py:477

commit v7 on v6

--- a/solution.py
+++ b/solution.py
@@ -199,13 +199,13 @@
         out_copies = [
             [
                 pltpu.make_async_copy(
-                    out_ref.at[e, :, pl.ds(part * 16, 16), :],
-                    out_hbm.at[e, :, pl.ds(part * 16, 16), :],
+                    out_ref.at[e, :, pl.ds(part * 8, 8), :],
+                    out_hbm.at[e, :, pl.ds(part * 8, 8), :],
                     sems.at[10 + 2 * part + e],
                 )
                 for e in range(2)
             ]
-            for part in range(2)
+            for part in range(4)
         ]
         padded_ref = out_ref.reshape(2 * 32 * PITCH, 128)
     else:
@@ -251,13 +251,13 @@
                 out_ref[place, :] = mine
         return carry
 
-    for part in range(2):
-        lax.fori_loop(part * 16, part * 16 + 16, second_step, 0, unroll=UNROLL)
+    for part in range(4):
+        lax.fori_loop(part * 8, part * 8 + 8, second_step, 0, unroll=8)
         if chunk:
             for copy in out_copies[part]:
                 copy.start()
     if chunk:
-        for copy in out_copies[0] + out_copies[1]:
+        for copy in sum(out_copies, []):
             copy.wait()
 
 
@@ -275,7 +275,7 @@
             pltpu.VMEM(second.shape, jnp.bfloat16),
             pltpu.VMEM((POINTS, 128), jnp.float32),
             pltpu.VMEM((32 * PITCH_BACK, 128), jnp.float32),
-            pltpu.SemaphoreType.DMA((14,)),
+            pltpu.SemaphoreType.DMA((18,)),
         ]
         + [
             pltpu.VMEM((POINTS, 128), jnp.float32),

time: 149 us -> 149 us (level)
  no operation moved by 1% of the time
where the time goes in v7:
time: 149 us; the launch traced here: 148 us
  waiting for transfers between devices  70.3 us (47%)
  Pallas kernels  48.4 us (32%)
  starting transfers between devices  26.8 us (18%)
  local copies, waits for them, and re-layouts  2.66 us (2%)
    all_to_all x4, waiting for transfers between devices, exchange(): moved = lax.all_to_all(parts, AXES, split_axis=0, concat_axis=0, tiled=True)  70.3 us
    all_to_all x4, starting transfers between devices, exchange(): moved = lax.all_to_all(parts, AXES, split_axis=0, concat_axis=0, tiled=True)  26.8 us
    pallas_call x2, Pallas kernels, product(): pl.pallas_call(product_kernel, grid=(PER // STEP,), in_specs=[pl.BlockSpe...  25.6 us
    pallas_call x2, Pallas kernels, forward(): pl.pallas_call(functools.partial(forward_kernel, [tile for _, tile in col...  12.1 us
    pallas_call x2, Pallas kernels, backward(): pl.pallas_call(functools.partial(backward_kernel, chunk), in_specs=[ANYWH...  6.85 us
    pallas_call x1, Pallas kernels, weights(): pl.pallas_call(weights_kernel, grid=(PER // STEP,), in_specs=[pl.BlockSpe...  3.81 us
  transfers between devices with their start and end apart: 4, of which 4 were waited for; matrix products, arithmetic and copies ran while one was open for 0% of the time, Pallas kernels for 25%

profile of v7, /device:TPU:1, one launch (start us, length us, event | category | flops | bytes accessed | tf_op | source)
XLA Modules:
  0.0 148.4 jit_solution(15749804565337548559)
XLA Ops:
  0.0 6.8 %forward.3 = f32[2048,384]{1,0:T(8,128)} custom-call(bf16[32,192,96]{2,1,0:T(8,128)(2,1)} %constant.44.clone.first_hbm, bf16[96,96]{1,0:T(8,128)(2,1)} %constant.45.clone.second_hbm, f32[32,32,512]{2,1,0:T(8,128)} %bitcast.21, f32[32,32,512]{2,1,0:T(8,128)} %bitcast.22, f32[32,32,128]{2,1,0:T(8,128)} %bitcast.25), custom_call_target="tpu_custom_call" | custom-call | flops 8999999488 | bytes 4718592 | tf_op jit(solution)/shard_map/forward/pallas_call | solution.py:174
  6.8 11.5 %all-to-all-start.1 = ((f32[128,16,384]{2,1,0:T(8,128)}), f32[128,16,384]{2,1,0:T(8,128)S(1)}, u32[]{:S(2)}, u32[]{:S(2)}) async-start(f32[128,16,384]{2,1,0:T(8,128)} %bitcast.17), calls=%async_computation.1 | async-start | bytes 6291456 | tf_op jit(solution)/shard_map/all_to_all | solution.py:477
  18.3 5.3 %forward.2 = f32[2048,256]{1,0:T(8,128)} custom-call(bf16[32,192,96]{2,1,0:T(8,128)(2,1)} %constant.44.clone.first_hbm, bf16[96,96]{1,0:T(8,128)(2,1)} %constant.45.clone.second_hbm, f32[32,32,512]{2,1,0:T(8,128)} %bitcast.23, f32[32,32,512]{2,1,0:T(8,128)} %bitcast.24), custom_call_target="tpu_custom_call" | custom-call | flops 6000000000 | bytes 3145728 | tf_op jit(solution)/shard_map/forward/pallas_call | solution.py:174
  23.6 36.2 %all-to-all-done.1 = f32[128,16,384]{2,1,0:T(8,128)S(1)} async-done(((f32[128,16,384]{2,1,0:T(8,128)}), f32[128,16,384]{2,1,0:T(8,128)S(1)}, u32[]{:S(2)}, u32[]{:S(2)}) %all-to-all-start.1) | async-done | bytes 3145760 | tf_op jit(solution)/shard_map/all_to_all | solution.py:477
  59.8 0.0 copy-start
  59.8 5.9 %all-to-all-start = ((f32[128,16,256]{2,1,0:T(8,128)}), f32[128,16,256]{2,1,0:T(8,128)}, u32[]{:S(2)}, u32[]{:S(2)}) async-start(f32[128,16,256]{2,1,0:T(8,128)} %bitcast.18), calls=%async_computation | async-start | bytes 4194304 | tf_op jit(solution)/shard_map/all_to_all | solution.py:477
  65.8 0.0 copy-done
  65.8 3.8 %weights.1.refs_2_ = bf16[16,256,768]{2,1,0:T(8,128)(2,1)S(1)} custom-call(f32[2048,384]{1,0:T(8,128)S(1)} %bitcast.12), custom_call_target="tpu_custom_call" | custom-call | flops 3000000000 | bytes 7340032 | tf_op jit(solution)/shard_map/weights/pallas_call | solution.py:335
  69.6 0.0 copy-start.2
  69.7 2.7 %copy-done.2 = bf16[16,256,768]{2,1,0:T(8,128)(2,1)} copy-done((bf16[16,256,768]{2,1,0:T(8,128)(2,1)}, bf16[16,256,768]{2,1,0:T(8,128)(2,1)S(1)}, u32[]{:S(2)}) %copy-start.2) | copy-done | bytes 6291480
  72.3 12.8 %product.3 = f32[2048,128]{1,0:T(8,128)} custom-call(f32[1]{0:T(128)} %bitcast.sign_ref, f32[2048,384]{1,0:T(8,128)} %bitcast.13, f32[2048,384]{1,0:T(8,128)} %bitcast.14, bf16[16,256,768]{2,1,0:T(8,128)(2,1)} %copy-done.2), custom_call_target="tpu_custom_call" | custom-call | flops 12000000000 | bytes 9437184 | tf_op jit(solution)/shard_map/product/pallas_call | solution.py:457
  85.1 10.9 %all-to-all-done = f32[128,16,256]{2,1,0:T(8,128)} async-done(((f32[128,16,256]{2,1,0:T(8,128)}), f32[128,16,256]{2,1,0:T(8,128)}, u32[]{:S(2)}, u32[]{:S(2)}) %all-to-all-start) | async-done | bytes 2097184 | tf_op jit(solution)/shard_map/all_to_all | solution.py:477
  96.0 4.6 %all-to-all-start.3 = ((f32[128,16,128]{2,1,0:T(8,128)}), f32[128,16,128]{2,1,0:T(8,128)S(1)}, u32[]{:S(2)}, u32[]{:S(2)}) async-start(f32[128,16,128]{2,1,0:T(8,128)} %bitcast.19), calls=%async_computation.3 | async-start | bytes 2097152 | tf_op jit(solution)/shard_map/all_to_all | solution.py:477
  100.7 12.8 %product.2 = f32[2048,128]{1,0:T(8,128)} custom-call(f32[1]{0:T(128)} %bitcast.sign_ref, f32[2048,256]{1,0:T(8,128)} %bitcast.3.refs_0_.refs_1_, f32[2048,256]{1,0:T(8,128)} %bitcast.3.refs_0_.refs_1_, bf16[16,256,768]{2,1,0:T(8,128)(2,1)} %copy-done.2), custom_call_target="tpu_custom_call" | custom-call | flops 12000000000 | bytes 9437184 | tf_op jit(solution)/shard_map/product/pallas_call | solution.py:457
  113.5 0.0 copy-start.1
  113.5 6.7 %all-to-all-done.3 = f32[128,16,128]{2,1,0:T(8,128)S(1)} async-done(((f32[128,16,128]{2,1,0:T(8,128)}), f32[128,16,128]{2,1,0:T(8,128)S(1)}, u32[]{:S(2)}, u32[]{:S(2)}) %all-to-all-start.3) | async-done | bytes 1048608 | tf_op jit(solution)/shard_map/all_to_all | solution.py:477
  120.2 4.7 %all-to-all-start.2 = ((f32[128,16,128]{2,1,0:T(8,128)}), f32[128,16,128]{2,1,0:T(8,128)S(1)}, u32[]{:S(2)}, u32[]{:S(2)}) async-start(f32[128,16,128]{2,1,0:T(8,128)} %bitcast.20), calls=%async_computation.2 | async-start | bytes 2097152 | tf_op jit(solution)/shard_map/all_to_all | solution.py:477
  124.9 0.0 copy-done.1
  124.9 3.0 %backward.2.refs_0_ = f32[2048,128]{1,0:T(8,128)S(1)} custom-call(bf16[64,96,96]{2,1,0:T(8,128)(2,1)} %constant.46.clone.first_hbm, bf16[96,192]{1,0:T(8,128)(2,1)S(1)} %copy-done.1, f32[2048,128]{1,0:T(8,128)S(1)} %bitcast.15), custom_call_target="tpu_custom_call" | custom-call | flops 5000000000 | bytes 3145728 | tf_op jit(solution)/shard_map/backward/pallas_call | solution.py:267
  127.9 16.5 %all-to-all-done.2 = f32[128,16,128]{2,1,0:T(8,128)S(1)} async-done(((f32[128,16,128]{2,1,0:T(8,128)}), f32[128,16,128]{2,1,0:T(8,128)S(1)}, u32[]{:S(2)}, u32[]{:S(2)}) %all-to-all-start.2) | async-done | bytes 1048608 | tf_op jit(solution)/shard_map/all_to_all | solution.py:477
  144.4 3.8 %backward.3 = f32[2,32,32,128]{3,2,1,0:T(8,128)} custom-call(bf16[64,96,96]{2,1,0:T(8,128)(2,1)} %constant.46.clone.first_hbm, bf16[96,192]{1,0:T(8,128)(2,1)S(1)} %copy-done.1, f32[2048,128]{1,0:T(8,128)S(1)} %bitcast.16, f32[2048,128]{1,0:T(8,128)S(1)} %backward.2.refs_0_), custom_call_target="tpu_custom_call" | custom-call | flops 5000000000 | bytes 3145728 | tf_op jit(solution)/shard_map/backward/pallas_call | solution.py:267
Async XLA Ops:
  6.8 53.0 %all-to-all-start.1 = ((f32[128,16,384]{2,1,0:T(8,128)}), f32[128,16,384]{2,1,0:T(8,128)S(1)}, u32[]{:S(2)}, u32[]{:S(2)}) async-start(f32[128,16,384]{2,1,0:T(8,128)} %bitcast.17), calls=%async_computation.1 | async-start | bytes 6291456 | tf_op jit(solution)/shard_map/all_to_all | solution.py:477
  59.8 6.0 %copy-start = (f32[128,16,384]{2,1,0:T(8,128)}, f32[128,16,384]{2,1,0:T(8,128)S(1)}, u32[]{:S(2)}) copy-start(f32[128,16,384]{2,1,0:T(8,128)S(1)} %all-to-all-done.1) | copy-start | bytes 9437188
  59.8 36.2 %all-to-all-start = ((f32[128,16,256]{2,1,0:T(8,128)}), f32[128,16,256]{2,1,0:T(8,128)}, u32[]{:S(2)}, u32[]{:S(2)}) async-start(f32[128,16,256]{2,1,0:T(8,128)} %bitcast.18), calls=%async_computation | async-start | bytes 4194304 | tf_op jit(solution)/shard_map/all_to_all | solution.py:477
  69.6 2.7 %copy-start.2 = (bf16[16,256,768]{2,1,0:T(8,128)(2,1)}, bf16[16,256,768]{2,1,0:T(8,128)(2,1)S(1)}, u32[]{:S(2)}) copy-start(bf16[16,256,768]{2,1,0:T(8,128)(2,1)S(1)} %weights.1.refs_2_) | copy-start | bytes 18874372
  96.0 24.2 %all-to-all-start.3 = ((f32[128,16,128]{2,1,0:T(8,128)}), f32[128,16,128]{2,1,0:T(8,128)S(1)}, u32[]{:S(2)}, u32[]{:S(2)}) async-start(f32[128,16,128]{2,1,0:T(8,128)} %bitcast.19), calls=%async_computation.3 | async-start | bytes 2097152 | tf_op jit(solution)/shard_map/all_to_all | solution.py:477
  113.5 11.4 %copy-start.1 = (bf16[96,192]{1,0:T(8,128)(2,1)S(1)}, bf16[96,192]{1,0:T(8,128)(2,1)}, u32[]{:S(2)}) copy-start(bf16[96,192]{1,0:T(8,128)(2,1)} %constant.47.clone.second_hbm) | copy-start | bytes 110596
  120.2 24.2 %all-to-all-start.2 = ((f32[128,16,128]{2,1,0:T(8,128)}), f32[128,16,128]{2,1,0:T(8,128)S(1)}, u32[]{:S(2)}, u32[]{:S(2)}) async-start(f32[128,16,128]{2,1,0:T(8,128)} %bitcast.20), calls=%async_computation.2 | async-start | bytes 2097152 | tf_op jit(solution)/shard_map/all_to_all | solution.py:477
